TPU v7x, 32 devices: a whole 2x2x4 slice. The times are simulated.
32 devices in a mesh: batch: 16 (over z, y, x), tower: 2 (over core).
Axes of the slice: x: 2, y: 2, z: 4, core: 2. Of those that a mesh axis runs over, the one named last changes fastest.
Arguments:
- crop_maps: bfloat16 [512, 2, 13, 13, 384], P(('batch', 'tower')), may hold values from -6 to 6
- cotangent: bfloat16 [512, 2, 4096], P('batch', None, 'tower'), may hold values from -48 to 48
- crop_counts: int32 [256], P('batch'), may hold values from 1 to 2, as said below
- filter_weight: float32 [6912, 256], P(('batch', 'tower')), may hold values from -0.109375 to 0.109375
- filter_first: float32 [6912, 256], P(('batch', 'tower')), may hold values from -640 to 640
- filter_second: float32 [6912, 256], P(('batch', 'tower')), may hold values from 13652.503 to 54610.01
- conv_filter_bias: float32 [512], P(('batch', 'tower')), may hold values from -0.625 to 0.625
- conv_filter_bias_mean: float32 [512], P(('batch', 'tower')), may hold values from -640 to 640
- conv_filter_bias_variance: float32 [512], P(('batch', 'tower')), may hold values from 13652.503 to 54610.01
- pool_stitch: float32 [1024], P(('batch', 'tower')), may hold values from 0.15 to 1
- pool_stitch_first: float32 [1024], P(('batch', 'tower')), may hold values from -1280 to 1280
- pool_stitch_second: float32 [1024], P(('batch', 'tower')), may hold values from 55296 to 221184
- dense_weight: float32 [2, 9216, 4096], P('tower', 'batch'), may hold values from -0.125 to 0.125
- dense_weight_first: float32 [2, 9216, 4096], P('tower', 'batch'), may hold values from -160 to 160
- dense_weight_second: float32 [2, 9216, 4096], P('tower', 'batch'), may hold values from 864 to 3456
- dense_bias: float32 [2, 4096], P('tower'), may hold values from -0.625 to 0.625
- dense_bias_first: float32 [2, 4096], P('tower'), may hold values from -512 to 512
- dense_bias_second: float32 [2, 4096], P('tower'), may hold values from 7104 to 28416
- dense_stitch: float32 [2, 2, 4096], P(None, None, 'tower'), may hold values from 0.15 to 1
- dense_stitch_first: float32 [2, 2, 4096], P(None, None, 'tower'), may hold values from -448 to 448
- dense_stitch_second: float32 [2, 2, 4096], P(None, None, 'tower'), may hold values from 4992 to 19968
Outputs:
- stitched: bfloat16 [512, 2, 4096], P('batch', None, 'tower')
- input_grad: bfloat16 [512, 2, 13, 13, 384], P(('batch', 'tower'))
- new_filter_weight: float32 [6912, 256], P(('batch', 'tower'))
- new_filter_first: float32 [6912, 256], P(('batch', 'tower'))
- new_filter_second: float32 [6912, 256], P(('batch', 'tower'))
- filter_copy: bfloat16 [6912, 256], P(('batch', 'tower'))
- new_filter_bias: float32 [512], P(('batch', 'tower'))
- new_filter_bias_first: float32 [512], P(('batch', 'tower'))
- new_filter_bias_second: float32 [512], P(('batch', 'tower'))
- new_pool_stitch: float32 [1024], P(('batch', 'tower'))
- new_pool_stitch_first: float32 [1024], P(('batch', 'tower'))
- new_pool_stitch_second: float32 [1024], P(('batch', 'tower'))
- new_dense_weight: float32 [2, 9216, 4096], P('tower', 'batch')
- new_dense_first: float32 [2, 9216, 4096], P('tower', 'batch')
- new_dense_second: float32 [2, 9216, 4096], P('tower', 'batch')
- dense_copy: bfloat16 [2, 9216, 4096], P('tower', 'batch')
- new_dense_bias: float32 [2, 4096], P('tower')
- new_dense_bias_first: float32 [2, 4096], P('tower')
- new_dense_bias_second: float32 [2, 4096], P('tower')
- new_dense_stitch: float32 [2, 2, 4096], P(None, None, 'tower')
- new_dense_stitch_first: float32 [2, 2, 4096], P(None, None, 'tower')
- new_dense_stitch_second: float32 [2, 2, 4096], P(None, None, 'tower')
Inputs may be any that keep to these rules, and one draw needn't show every extreme that they name: `crop_counts`: block b of 16 crop slots holds the crops of images b * 8 to b * 8 + 7 in order, then empty slots; in every draw some block is full.
All inputs are finite; a program needn't handle non-finite values.
Results may differ from a plain program's by a relative error of at most 0.0093.
Values may be sent and summed in bfloat16 or wider, within the bound.
No kernel may reach another device: no remote copies, remote signals or barrier semaphores. Data moves between devices by JAX's collectives and lax.ppermute only.
A program may use at most 448 MiB of HBM per device.

v0:
```python
import jax
import jax.numpy as jnp
from jax import lax
from jax.sharding import PartitionSpec as P

STEP = 10


BETA_ONE = 0.5
BETA_TWO = 0.5
EPSILON = 1e-08
DECAY = 0.01
RATE_FILTER = 0.02
RATE_DENSE = 0.02
BIAS_LEARN_RATE = 0.05
RATE_STITCH = 0.2


def smooth_gate(values):
    return jax.nn.gelu(values, approximate=True)


def gate_slope(values):
    return jax.vjp(smooth_gate, values)[1](jnp.ones_like(values))[0]


def stitch_mix(weights, values):
    extra = values.ndim - 3
    shaped = weights.reshape((1, 2, 2) + (1,) * extra + (weights.shape[-1],))
    return jnp.sum(shaped * values[:, None], axis=2)


def stitch_grad(gradient_tuple, values):
    product = gradient_tuple[:, :, None] * values[:, None, :]
    axes = (0,) + tuple(range(3, product.ndim - 1))
    return jnp.sum(product, axis=axes)


def pool_mean(active):
    pooled_side = (active.shape[2] - 1) // 2
    total = jnp.zeros(active.shape[:2] + (pooled_side, pooled_side, active.shape[4]), jnp.float32)
    for offset in range(9):
        row_start = offset // 3
        col_start = offset % 3
        total = (
            total
            + active[
                :,
                :,
                row_start : row_start + 2 * pooled_side - 1 : 2,
                col_start : col_start + 2 * pooled_side - 1 : 2,
                :,
            ]
        )
    return total / 9.0


def pool_spread(gradient_tuple, full_side):
    pooled_side = gradient_tuple.shape[2]
    scaled = gradient_tuple / 9.0
    total = jnp.zeros(
        gradient_tuple.shape[:2] + (full_side, full_side, gradient_tuple.shape[4]), jnp.float32
    )
    for offset in range(9):
        row_start = offset // 3
        col_start = offset % 3
        row_end = full_side - row_start - (2 * pooled_side - 1)
        col_end = full_side - col_start - (2 * pooled_side - 1)
        total = total + lax.pad(
            scaled,
            jnp.float32(0),
            ((0, 0, 0), (0, 0, 0), (row_start, row_end, 1), (col_start, col_end, 1), (0, 0, 0)),
        )
    return total


def decoupled_adam_step(master, first, second, grad, rate, decay):
    first_new = BETA_ONE * first + (1.0 - BETA_ONE) * grad
    second_new = BETA_TWO * second + (1.0 - BETA_TWO) * grad * grad
    first_hat = first_new / (1.0 - BETA_ONE**STEP)
    second_hat = second_new / (1.0 - BETA_TWO**STEP)
    master_new = master - rate * (first_hat / (jnp.sqrt(second_hat) + EPSILON) + decay * master)
    return (master_new, first_new, second_new)


def local(
    crop_maps,
    cotangent,
    crop_counts,
    filter_weight,
    filter_first,
    filter_second,
    conv_filter_bias,
    conv_filter_bias_mean,
    conv_filter_bias_variance,
    pool_stitch,
    pool_stitch_first,
    pool_stitch_second,
    dense_weight,
    dense_weight_first,
    dense_weight_second,
    dense_bias,
    dense_bias_first,
    dense_bias_second,
    dense_stitch,
    dense_stitch_first,
    dense_stitch_second,
):
    block_rows = crop_maps.shape[0]
    side = crop_maps.shape[2]
    in_width = crop_maps.shape[4]
    totals = jnp.sum(crop_counts.reshape(2, -1), axis=1)
    slots = jnp.arange(block_rows, dtype=jnp.int32)
    mask = (slots[None, :] < totals[:, None]).astype(jnp.float32).reshape(-1)
    filter_full, bias_full, stitch_full = (
        lax.all_gather(filter_weight.astype(jnp.bfloat16), ("batch", "tower"), axis=0, tiled=True),
        lax.all_gather(
            conv_filter_bias.astype(jnp.bfloat16), ("batch", "tower"), axis=0, tiled=True
        ),
        lax.all_gather(pool_stitch.astype(jnp.bfloat16), ("batch", "tower"), axis=0, tiled=True),
    )
    out_width = filter_full.shape[1]
    filters = filter_full.reshape(2, 9, in_width, out_width)
    biases = bias_full.astype(jnp.float32).reshape(2, out_width)
    pool_low = stitch_full.astype(jnp.float32).reshape(2, 2, out_width)
    padded = jnp.pad(crop_maps, ((0, 0), (0, 0), (1, 1), (1, 1), (0, 0)))
    conv = jnp.zeros((block_rows, 2, side, side, out_width), jnp.float32)
    for offset in range(9):
        row_start = offset // 3
        col_start = offset % 3
        window = padded[:, :, row_start : row_start + side, col_start : col_start + side, :]
        conv = conv + jnp.einsum(
            "ntyxc,tco->ntyxo", window, filters[:, offset], preferred_element_type=jnp.float32
        )
    conv = conv + biases[None, :, None, None, :]
    pooled = pool_mean(smooth_gate(conv))
    pooled_side = pooled.shape[2]
    mixed = stitch_mix(pool_low, pooled).astype(jnp.bfloat16).reshape(block_rows, 2, -1)
    features = lax.all_to_all(mixed, "tower", split_axis=1, concat_axis=0, tiled=True)[:, 0, :]
    feature_width = features.shape[1]
    pair_rows = features.shape[0]
    dense_low = dense_weight[0].astype(jnp.bfloat16)
    unit_width = dense_low.shape[1]
    columns = features
    hidden = jnp.dot(
        columns,
        lax.all_gather(dense_low, "batch", axis=0, tiled=True),
        preferred_element_type=jnp.float32,
    )
    hidden = hidden + dense_bias
    active = smooth_gate(hidden).astype(jnp.bfloat16).reshape(pair_rows, 1, 2, unit_width // 2)
    units = lax.all_to_all(active, "tower", split_axis=2, concat_axis=1, tiled=True)[:, :, 0, :]
    units_float = units.astype(jnp.float32)
    stitched = (stitch_mix(dense_stitch, units_float) * mask[:, None, None]).astype(jnp.bfloat16)
    grad_out = cotangent.astype(jnp.float32) * mask[:, None, None]
    grad_dense_stitch = stitch_grad(grad_out, units_float)
    grad_units = stitch_mix(jnp.swapaxes(dense_stitch, 0, 1), grad_out).astype(jnp.bfloat16)
    grad_active = lax.all_to_all(
        grad_units.reshape(pair_rows, 2, 1, -1), "tower", split_axis=1, concat_axis=2, tiled=True
    ).reshape(pair_rows, unit_width)
    grad_hidden = (grad_active.astype(jnp.float32) * gate_slope(hidden)).astype(jnp.bfloat16)
    grad_dense_bias = jnp.sum(grad_hidden.astype(jnp.float32), axis=0)
    grad_features = jnp.einsum(
        "nu,ru->nr",
        grad_hidden,
        lax.all_gather(dense_low, "batch", axis=0, tiled=True),
        preferred_element_type=jnp.float32,
    ).astype(jnp.bfloat16)
    columns = features
    grad_dense_weight = lax.psum_scatter(
        jnp.einsum("nr,nu->ru", columns, grad_hidden, preferred_element_type=jnp.float32),
        "batch",
        scatter_dimension=0,
        tiled=True,
    )
    grad_dense_stitch, grad_dense_bias = lax.psum((grad_dense_stitch, grad_dense_bias), "batch")
    grad_mixed = lax.all_to_all(
        grad_features.reshape(pair_rows, 1, feature_width),
        "tower",
        split_axis=0,
        concat_axis=1,
        tiled=True,
    )
    grad_mixed = grad_mixed.astype(jnp.float32).reshape(
        block_rows, 2, pooled_side, pooled_side, out_width
    )
    grad_pool_stitch = stitch_grad(grad_mixed, pooled)
    grad_pooled = stitch_mix(jnp.swapaxes(pool_low, 0, 1), grad_mixed)
    grad_conv = (pool_spread(grad_pooled, side) * gate_slope(conv)).astype(jnp.bfloat16)
    grad_filter_bias = jnp.sum(grad_conv.astype(jnp.float32), axis=(0, 2, 3))
    weight_terms = []
    input_total = jnp.zeros((block_rows, 2, side + 2, side + 2, in_width), jnp.float32)
    for offset in range(9):
        row_start = offset // 3
        col_start = offset % 3
        window = padded[:, :, row_start : row_start + side, col_start : col_start + side, :]
        weight_terms.append(
            jnp.einsum("ntyxc,ntyxo->tco", window, grad_conv, preferred_element_type=jnp.float32)
        )
        backward_part = jnp.einsum(
            "ntyxo,tco->ntyxc", grad_conv, filters[:, offset], preferred_element_type=jnp.float32
        )
        input_total = input_total + lax.pad(
            backward_part,
            jnp.float32(0),
            (
                (0, 0, 0),
                (0, 0, 0),
                (row_start, 2 - row_start, 0),
                (col_start, 2 - col_start, 0),
                (0, 0, 0),
            ),
        )
    input_grad = input_total[:, :, 1 : side + 1, 1 : side + 1, :].astype(jnp.bfloat16)
    grad_filter_weight = jnp.stack(weight_terms, axis=1).reshape(-1, out_width)
    filter_sums, filter_bias_sums, pool_sums = (
        lax.psum_scatter(grad_filter_weight, ("batch", "tower"), scatter_dimension=0, tiled=True),
        lax.psum_scatter(
            grad_filter_bias.reshape(-1), ("batch", "tower"), scatter_dimension=0, tiled=True
        ),
        lax.psum_scatter(
            grad_pool_stitch.reshape(-1), ("batch", "tower"), scatter_dimension=0, tiled=True
        ),
    )
    updated_conv_weight, updated_conv_weight_mean, updated_conv_weight_variance = (
        decoupled_adam_step(
            filter_weight, filter_first, filter_second, filter_sums, RATE_FILTER, DECAY
        )
    )
    updated_conv_bias, updated_conv_bias_mean, updated_conv_bias_variance = decoupled_adam_step(
        conv_filter_bias,
        conv_filter_bias_mean,
        conv_filter_bias_variance,
        filter_bias_sums,
        BIAS_LEARN_RATE,
        0.0,
    )
    updated_pooling_stitch, updated_pooling_stitch_mean, updated_pooling_stitch_variance = (
        decoupled_adam_step(
            pool_stitch, pool_stitch_first, pool_stitch_second, pool_sums, RATE_STITCH, 0.0
        )
    )
    updated_dense_weight, updated_dense_weight_mean, updated_dense_weight_variance = (
        decoupled_adam_step(
            dense_weight,
            dense_weight_first,
            dense_weight_second,
            grad_dense_weight[None],
            RATE_DENSE,
            DECAY,
        )
    )
    updated_dense_bias, updated_dense_bias_mean, updated_dense_bias_variance = decoupled_adam_step(
        dense_bias, dense_bias_first, dense_bias_second, grad_dense_bias[None], BIAS_LEARN_RATE, 0.0
    )
    updated_dense_stitch, updated_dense_stitch_mean, updated_dense_stitch_variance = (
        decoupled_adam_step(
            dense_stitch,
            dense_stitch_first,
            dense_stitch_second,
            grad_dense_stitch,
            RATE_STITCH,
            0.0,
        )
    )
    return (
        stitched,
        input_grad,
        updated_conv_weight,
        updated_conv_weight_mean,
        updated_conv_weight_variance,
        updated_conv_weight.astype(jnp.bfloat16),
        updated_conv_bias,
        updated_conv_bias_mean,
        updated_conv_bias_variance,
        updated_pooling_stitch,
        updated_pooling_stitch_mean,
        updated_pooling_stitch_variance,
        updated_dense_weight,
        updated_dense_weight_mean,
        updated_dense_weight_variance,
        updated_dense_weight.astype(jnp.bfloat16),
        updated_dense_bias,
        updated_dense_bias_mean,
        updated_dense_bias_variance,
        updated_dense_stitch,
        updated_dense_stitch_mean,
        updated_dense_stitch_variance,
    )


def solution(mesh):
    in_specs = (
        P(("batch", "tower"), None, None, None, None),
        P("batch", None, "tower"),
        P("batch"),
        P(("batch", "tower"), None),
        P(("batch", "tower"), None),
        P(("batch", "tower"), None),
        P(("batch", "tower")),
        P(("batch", "tower")),
        P(("batch", "tower")),
        P(("batch", "tower")),
        P(("batch", "tower")),
        P(("batch", "tower")),
        P("tower", "batch", None),
        P("tower", "batch", None),
        P("tower", "batch", None),
        P("tower", None),
        P("tower", None),
        P("tower", None),
        P(None, None, "tower"),
        P(None, None, "tower"),
        P(None, None, "tower"),
    )
    out_specs = (
        P("batch", None, "tower"),
        P(("batch", "tower"), None, None, None, None),
        P(("batch", "tower"), None),
        P(("batch", "tower"), None),
        P(("batch", "tower"), None),
        P(("batch", "tower"), None),
        P(("batch", "tower")),
        P(("batch", "tower")),
        P(("batch", "tower")),
        P(("batch", "tower")),
        P(("batch", "tower")),
        P(("batch", "tower")),
        P("tower", "batch", None),
        P("tower", "batch", None),
        P("tower", "batch", None),
        P("tower", "batch", None),
        P("tower", None),
        P("tower", None),
        P("tower", None),
        P(None, None, "tower"),
        P(None, None, "tower"),
        P(None, None, "tower"),
    )
    return jax.shard_map(local, mesh=mesh, in_specs=in_specs, out_specs=out_specs, check_vma=False)
```

profile of v0, /device:TPU:0, one launch (start us, length us, event | category | flops | bytes accessed | tf_op | source)
XLA Modules:
  0.0 3391.5 jit_solution(14733489296404303744)
XLA Ops:
  7.2 1.6 convert_element_type.109
  8.9 6.6 convert_element_type.113
  17.0 42.4 %all-reduce.25 = (bf16[1024]{0:T(1024)(128)(2,1)S(1)}, bf16[512]{0:T(512)(128)(2,1)S(1)}) all-reduce(bf16[1024]{0:T(1024)(128)(2,1)S(1)} %dynamic-update-slice, bf16[512]{0:T(512)(128)(2,1)S(1)} %dynamic-update-slice.1), channel_id=1, replica_groups=mesh['batch'=16,'tower'=2] {'batch','tower'}, use_global_device_ids=true, to_apply=%add.19 | all-reduce | flops 1536 | bytes 6144
  59.5 2.8 copy.149
  62.4 11.1 pad_slice_fusion
  74.5 6.4 fusion.113
  80.8 5.5 fusion.112
  86.3 4.6 fusion.111
  91.0 4.6 fusion.110
  95.6 4.5 fusion.109
  100.0 4.4 fusion.108
  104.4 4.8 fusion.106
  109.2 4.5 fusion.107
  113.7 19.7 multiply_multiply_fusion.3
  133.4 5.5 add_multiply_fusion
  139.3 1.5 convert_element_type.112
  140.8 5.3 all_to_all.42
  146.1 678.5 %all-gather.6.cloned.1.call-done = bf16[1,9216,4096]{2,1,0:T(8,128)(2,1)} async-done(((bf16[1,576,4096]{2,1,0:T(8,128)(2,1)}), bf16[1,9216,4096]{2,1,0:T(8,128)(2,1)}) %all-gather.6.cloned.1.call-update) | async-done | bytes 75497488 | tf_op jit(solution)/shard_map/all_gather | solution.py:147
  824.5 27.5 multiply_convert_fusion.1
  852.4 3.9 all_to_all.43
  856.4 1.1 multiply_reduce_fusion.3
  857.5 4.3 all_to_all.44
  864.1 29.6 fusion.7
  895.7 4.2 all_to_all.45
  900.5 1.2 copy.318
  901.7 1.9 reshape.151
  905.3 24.2 pad.67
  929.5 24.2 pad.66
  953.6 24.0 pad.65
  977.6 24.1 pad.64
  1001.7 24.0 pad.63
  1025.7 24.0 pad.62
  1049.7 24.0 pad.61
  1073.7 23.9 pad.59
  1097.7 24.1 pad.60
  1121.7 21.2 convert_reduce_fusion
  1142.9 4.1 fusion.53
  1147.0 1.8 fusion.59
  1149.2 1.8 fusion.65
  1151.4 1.8 fusion.71
  1153.6 1.8 fusion.47
  1155.7 1.8 fusion.77
  1157.9 1.8 fusion.83
  1160.1 2.0 fusion.89
  1162.3 1.8 fusion.95
  1164.1 3.6 copy.189
  1168.7 55.1 %fusion.147 = f32[9216,4096]{1,0:T(8,128)} fusion(bf16[32,9216]{1,0:T(8,128)(2,1)S(1)} %bitcast.301, bf16[32,4096]{1,0:T(8,128)(2,1)} %copy-done.13), kind=kOutput, calls=%fused_computation.175 | convolution fusion | flops 2415919104 | bytes 151846912 | tf_op jit(solution)/shard_map/nr,nu->ru/dot_general | solution.py:171
  1226.0 2.8 convolution_bitcast_fusion.5
  1228.7 1.6 convolution_bitcast_fusion.6
  1230.3 5.0 convolution_bitcast_fusion.7
  1235.3 5.0 convolution_bitcast_fusion.8
  1240.3 12.8 pad_add_fusion
  1253.1 5.0 convolution_bitcast_fusion
  1258.1 5.0 convolution_bitcast_fusion.1
  1263.0 5.0 convolution_bitcast_fusion.2
  1268.0 4.8 convolution_bitcast_fusion.3
  1272.8 4.9 convolution_bitcast_fusion.4
  1277.7 18.1 fusion.13
  1296.0 7.5 copy.192
  1303.5 41.4 %all-reduce.23 = (f32[512]{0:T(512)S(1)}, f32[1024]{0:T(1024)S(1)}) all-reduce(f32[512]{0:T(512)S(1)} %bitcast.315, f32[1024]{0:T(1024)S(1)} %bitcast.313), channel_id=4, replica_groups=mesh['batch'=16,'tower'=2] {'batch','tower'}, use_global_device_ids=true, to_apply=%region_7.8.clone | all-reduce | flops 1536 | bytes 12288
  1344.9 79.6 %all-reduce.24 = (f32[4096]{0:T(1024)S(1)}, f32[2,2,2048]{2,1,0:T(2,128)S(1)}) all-reduce(f32[4096]{0:T(1024)S(1)} %copy-done.22, f32[2,2,2048]{2,1,0:T(2,128)S(1)} %copy-done.21), channel_id=1, replica_groups=mesh['batch'=16,'tower'=2] {'batch'}, use_global_device_ids=true, to_apply=%region_12.13 | all-reduce | flops 12288 | bytes 98304 | tf_op jit(solution)/shard_map/psum | solution.py:176
  1427.2 1.9 fusion.145
  1429.1 1929.6 %reduce-scatter.5.cloned.1.call-done = f32[576,4096]{1,0:T(8,128)} async-done(((f32[9216,4096]{1,0:T(8,128)}), f32[576,4096]{1,0:T(8,128)}) %reduce-scatter.5.cloned.1.call-update) | async-done | bytes 9437200 | tf_op jit(solution)/shard_map/reduce_scatter | solution.py:170
  3358.7 26.1 fusion.139
  (133 shorter events, 18.3 us)
Async XLA Ops:
  7.2 67.3 %all-gather.4.cloned.1.call-start = ((), (), s32[]{:S(2)}) async-start(), calls=%async_computation.6 | async-start | bytes 3649536 | tf_op jit(solution)/shard_map/all_gather | solution.py:116
  8.9 815.7 %all-gather.6.cloned.1.call-start = ((), (), s32[]{:S(2)}) async-start(), calls=%async_computation.9 | async-start | bytes 80216064 | tf_op jit(solution)/shard_map/all_gather | solution.py:147
  15.5 0.7 copy-start.41
  15.5 1.0 copy-start.37
  15.5 1.0 copy-start.33
  15.5 44.0 %copy-start.16 = (f32[2,2,2048]{2,1,0:T(2,128)S(1)}, f32[2,2,2048]{2,1,0:T(2,128)}, u32[]{:S(2)}) copy-start(f32[2,2,2048]{2,1,0:T(2,128)} %param.39) | copy-start | bytes 98308
  15.5 1411.7 %reduce-scatter.3.cloned.1.call-start = ((), (), s32[]{:S(2)}) async-start(), calls=%async_computation.7 | async-start | bytes 7299072 | tf_op jit(solution)/shard_map/reduce_scatter | solution.py:217
  16.5 45.8 %copy-start.31 = (f32[32]{0:T(128)}, f32[32]{0:T(128)S(1)}, u32[]{:S(2)}) copy-start(f32[32]{0:T(128)S(1)} %reshape.149) | copy-start | bytes 388
  59.5 2.8 copy-start.18
  74.5 6.4 copy-start
  74.5 6.4 copy-start.2
  138.9 685.6 %copy-start.23 = (f32[1,4096]{1,0:T(1,128)S(1)}, f32[1,4096]{1,0:T(1,128)}, u32[]{:S(2)}) copy-start(f32[1,4096]{1,0:T(1,128)} %param.36) | copy-start | bytes 49156
  146.1 706.0 %copy-start.4 = (bf16[16,2,9216]{2,0,1:T(8,128)(2,1)}, bf16[16,2,9216]{2,0,1:T(8,128)(2,1)S(1)}, u32[]{:S(2)}) copy-start(bf16[16,2,9216]{2,0,1:T(8,128)(2,1)S(1)} %all_to_all.42) | copy-start | bytes 1769476
  863.4 0.7 copy-start.13
  1142.9 4.1 copy-start.12
  1147.0 2.2 copy-start.11
  1149.2 2.2 copy-start.10
  1151.4 2.2 copy-start.1
  1153.6 2.2 copy-start.9
  1155.7 2.2 copy-start.8
  1157.9 2.2 copy-start.7
  1160.1 2.2 copy-start.6
  1167.7 1.1 copy-start.5
  1167.7 2191.0 %reduce-scatter.5.cloned.1.call-start = ((), (), s32[]{:S(2)}) async-start(), calls=%async_computation.8 | async-start | bytes 160432128 | tf_op jit(solution)/shard_map/reduce_scatter | solution.py:170
  1223.8 1.0 copy-start.14
  1223.8 1.0 copy-start.32
  1226.0 2.8 copy-start.3
  1295.8 7.7 copy-start.30
  1295.8 7.7 copy-start.27
  1295.8 49.1 %copy-start.21 = (f32[2,2,2048]{2,1,0:T(2,128)S(1)}, f32[2,2,2048]{2,1,0:T(2,128)}, u32[]{:S(2)}) copy-start(f32[2,2,2048]{2,1,0:T(2,128)} %get-tuple-element.112) | copy-start | bytes 98308
  1295.8 49.1 %copy-start.22 = (f32[4096]{0:T(1024)S(1)}, f32[4096]{0:T(1024)}, u32[]{:S(2)}) copy-start(f32[4096]{0:T(1024)} %get-tuple-element.127) | copy-start | bytes 49156
  1295.8 128.7 %copy-start.34 = (f32[16]{0:T(128)S(1)}, f32[16]{0:T(128)}, u32[]{:S(2)}) copy-start(f32[16]{0:T(128)} %param.27) | copy-start | bytes 196
  1295.8 128.6 %copy-start.35 = (f32[16]{0:T(128)S(1)}, f32[16]{0:T(128)}, u32[]{:S(2)}) copy-start(f32[16]{0:T(128)} %param.28) | copy-start | bytes 196
  1295.8 128.6 %copy-start.36 = (f32[16]{0:T(128)S(1)}, f32[16]{0:T(128)}, u32[]{:S(2)}) copy-start(f32[16]{0:T(128)} %param.29) | copy-start | bytes 196
  1295.9 129.2 %copy-start.38 = (f32[32]{0:T(128)S(1)}, f32[32]{0:T(128)}, u32[]{:S(2)}) copy-start(f32[32]{0:T(128)} %param.30) | copy-start | bytes 388
  1295.9 129.2 %copy-start.39 = (f32[32]{0:T(128)S(1)}, f32[32]{0:T(128)}, u32[]{:S(2)}) copy-start(f32[32]{0:T(128)} %param.31) | copy-start | bytes 388
  1295.9 129.2 %copy-start.40 = (f32[32]{0:T(128)S(1)}, f32[32]{0:T(128)}, u32[]{:S(2)}) copy-start(f32[32]{0:T(128)} %param.32) | copy-start | bytes 388
  1295.9 129.8 %copy-start.17 = (f32[2,2,2048]{2,1,0:T(2,128)S(1)}, f32[2,2,2048]{2,1,0:T(2,128)}, u32[]{:S(2)}) copy-start(f32[2,2,2048]{2,1,0:T(2,128)} %param.39) | copy-start | bytes 98308
  1295.9 129.8 %copy-start.25 = (f32[2,2,2048]{2,1,0:T(2,128)S(1)}, f32[2,2,2048]{2,1,0:T(2,128)}, u32[]{:S(2)}) copy-start(f32[2,2,2048]{2,1,0:T(2,128)} %param.40) | copy-start | bytes 98308
  1295.9 129.8 %copy-start.26 = (f32[2,2,2048]{2,1,0:T(2,128)S(1)}, f32[2,2,2048]{2,1,0:T(2,128)}, u32[]{:S(2)}) copy-start(f32[2,2,2048]{2,1,0:T(2,128)} %param.41) | copy-start | bytes 98308
  1295.9 130.6 %copy-start.24 = (f32[1,4096]{1,0:T(1,128)S(1)}, f32[1,4096]{1,0:T(1,128)}, u32[]{:S(2)}) copy-start(f32[1,4096]{1,0:T(1,128)} %param.36) | copy-start | bytes 49156
  1295.9 130.6 %copy-start.28 = (f32[1,4096]{1,0:T(1,128)S(1)}, f32[1,4096]{1,0:T(1,128)}, u32[]{:S(2)}) copy-start(f32[1,4096]{1,0:T(1,128)} %param.37) | copy-start | bytes 49156
  1295.9 130.5 %copy-start.29 = (f32[1,4096]{1,0:T(1,128)S(1)}, f32[1,4096]{1,0:T(1,128)}, u32[]{:S(2)}) copy-start(f32[1,4096]{1,0:T(1,128)} %param.38) | copy-start | bytes 49156
  1296.0 131.3 %copy-start.15 = (f32[216,256]{1,0:T(8,128)S(1)}, f32[216,256]{1,0:T(8,128)}, u32[]{:S(2)}) copy-start(f32[216,256]{1,0:T(8,128)} %param.24) | copy-start | bytes 663556
  1296.0 131.3 %copy-start.19 = (f32[216,256]{1,0:T(8,128)S(1)}, f32[216,256]{1,0:T(8,128)}, u32[]{:S(2)}) copy-start(f32[216,256]{1,0:T(8,128)} %param.25) | copy-start | bytes 663556
  1296.0 131.2 %copy-start.20 = (f32[216,256]{1,0:T(8,128)S(1)}, f32[216,256]{1,0:T(8,128)}, u32[]{:S(2)}) copy-start(f32[216,256]{1,0:T(8,128)} %param.26) | copy-start | bytes 663556
Sparse Core Ops, SparseCore 0:
  11.5 62.9 all-gather.3
  77.9 746.5 all-gather.5
  1167.8 117.1 reduce-scatter.2
  1291.9 2066.7 reduce-scatter.4
where the time goes:
time: 3400 us; the launch traced here: 3390 us
  waiting for transfers between devices  2610 us (77%)
  local copies, waits for them, and re-layouts  257 us (8%)
  matrix products  229 us (7%)
  blocking collectives  181 us (5%)
  other arithmetic  101 us (3%)
    reduce_scatter x1, waiting for transfers between devices, local(): lax.psum_scatter(jnp.einsum('nr,nu->ru', columns, grad_hidden, preferred_...  1930 us
    all_gather x1, waiting for transfers between devices, local(): lax.all_gather(dense_low, 'batch', axis=0, tiled=True)  678 us
    pad x9, local copies, waits for them, and re-layouts, pool_spread(): lax.pad(scaled, jnp.float32(0), ((0, 0, 0), (0, 0, 0), (row_start, row_en...  216 us
    unnamed x2, blocking collectives  83.8 us
    psum x1, blocking collectives, local(): lax.psum((grad_dense_stitch, grad_dense_bias), 'batch')  79.6 us
  transfers between devices with their start and end apart: 4, of which 3 were waited for; matrix products, arithmetic and copies ran while one was open for 7% of the time, Pallas kernels for 0%

commit v1 on v0

v1 whole, which is shorter than its diff:
```python
import jax
import jax.numpy as jnp
from jax import lax
from jax.sharding import PartitionSpec as P

STEP = 10


BETA_ONE = 0.5
BETA_TWO = 0.5
EPSILON = 1e-08
DECAY = 0.01
RATE_FILTER = 0.02
RATE_DENSE = 0.02
BIAS_LEARN_RATE = 0.05
RATE_STITCH = 0.2


def smooth_gate(values):
    return jax.nn.gelu(values, approximate=True)


def gate_slope(values):
    return jax.vjp(smooth_gate, values)[1](jnp.ones_like(values))[0]


def pool_mean(active):
    pooled_side = (active.shape[1] - 1) // 2
    span = 2 * pooled_side - 1
    total = jnp.zeros((), jnp.float32)
    for row_start in range(3):
        for col_start in range(3):
            total = total + active[:, row_start : row_start + span : 2, col_start : col_start + span : 2]
    return total / 9.0


def pool_spread(gradient, full_side):
    scaled = gradient / 9.0
    for axis in (1, 2):
        even = jnp.concatenate([scaled, jnp.zeros_like(lax.slice_in_dim(scaled, 0, 1, axis=axis))], axis)
        shifted = jnp.concatenate([jnp.zeros_like(lax.slice_in_dim(scaled, 0, 1, axis=axis)), scaled], axis)
        pairs = jnp.stack([even + shifted, even], axis + 1)
        shape = list(scaled.shape)
        shape[axis] = 2 * shape[axis] + 2
        scaled = lax.slice_in_dim(pairs.reshape(shape), 0, full_side, axis=axis)
    return scaled


CUBE = 16


def cube():
    return lax.axis_size("batch") == CUBE


def hop(values, offset):
    return lax.ppermute(values, "batch", [(i, i ^ offset) for i in range(CUBE)])


def core_swap(values):
    return lax.ppermute(values, "tower", [(0, 1), (1, 0)])


def by_core(core, own, other):
    return jnp.where(
        core == 0,
        jnp.concatenate([own, other], axis=-1),
        jnp.concatenate([other, own], axis=-1),
    )


def plane_axes(level):
    return (1, 2) if level % 2 == 0 else (2, 1)


LEVELS = (3, 2, 1, 0)


def block_order(level):
    first, second = plane_axes(level)
    return [4 * level + offset for offset in (first, 3, 0, second)]


def sum_batch(values):
    if not cube():
        return lax.psum(values, "batch")
    for offset in (1, 2, 4, 8):
        values = values + hop(values, offset)
    return values


def gather_blocks(block):
    blocks = {}
    tops = {level: hop(block, 4 * level) if level else block for level in range(4)}
    for level in range(4):
        first, second = plane_axes(level)
        near = hop(tops[level], first)
        blocks[4 * level] = tops[level]
        blocks[4 * level + first] = near
        blocks[4 * level + second] = hop(tops[level], second)
        blocks[4 * level + 3] = hop(near, second)
    return blocks


def gather_packed(packed):
    if not cube():
        return lax.all_gather(packed, ("batch", "tower"), axis=0)
    chip, core = lax.axis_index("batch"), lax.axis_index("tower")
    own = jnp.zeros((CUBE,) + packed.shape, packed.dtype)
    for offset, block in gather_blocks(packed).items():
        own = lax.dynamic_update_slice(own, block[None], (chip ^ offset, 0, 0))
    other = core_swap(own)
    return jnp.where(
        core == 0, jnp.stack([own, other], axis=1), jnp.stack([other, own], axis=1)
    ).reshape((2 * CUBE,) + packed.shape)


def scatter_chunks(chunks, chip):
    if not cube():
        arrived = lax.all_to_all(chunks, "batch", split_axis=0, concat_axis=0, tiled=True)
        return [arrived.reshape(-1, chunks.shape[2])]
    parts = []
    for level in LEVELS:
        arrived = []
        for offset in block_order(level):
            chunk = lax.dynamic_index_in_dim(chunks, chip ^ offset, axis=0, keepdims=False)
            arrived.append(hop(chunk, offset) if offset else chunk)
        parts.append(jnp.concatenate(arrived))
    return parts


def return_chunks(parts, chip, rows):
    if not cube():
        blocks = parts[0].reshape(-1, rows, parts[0].shape[1])
        return lax.all_to_all(blocks, "batch", split_axis=0, concat_axis=0, tiled=True)
    chunks = jnp.zeros((CUBE, rows, parts[0].shape[1]), parts[0].dtype)
    for level, part in zip(LEVELS, parts):
        for place, offset in enumerate(block_order(level)):
            block = part[place * rows : (place + 1) * rows]
            block = hop(block, offset) if offset else block
            chunks = lax.dynamic_update_slice(chunks, block[None], (chip ^ offset, 0, 0))
    return chunks


def reduce_rows(parts, rows):
    if not cube():
        total = lax.psum_scatter(parts[0], "batch", scatter_dimension=0, tiled=True)
        return total.astype(jnp.float32)
    total = 0.0
    for level, part in zip(LEVELS, parts):
        first, second = plane_axes(level)
        kept = part[2 * rows :].astype(jnp.float32) + hop(part[: 2 * rows], first).astype(jnp.float32)
        kept = kept[:rows] + hop(kept[rows:].astype(jnp.bfloat16), second).astype(jnp.float32)
        if level:
            kept = hop(kept.astype(jnp.bfloat16), 4 * level).astype(jnp.float32)
        total = total + kept
    return total


def gather_rows(block):
    if not cube():
        return [lax.all_gather(block, "batch", axis=0, tiled=True)]
    blocks = gather_blocks(block)
    return [
        jnp.concatenate([blocks[offset] for offset in block_order(level)]) for level in LEVELS
    ]


def reduce_filters(grads, chip, core):
    own = lax.dynamic_index_in_dim(grads, core, axis=1, keepdims=False).astype(jnp.float32)
    other = lax.dynamic_index_in_dim(grads, 1 - core, axis=1, keepdims=False)
    pair = own + core_swap(other).astype(jnp.float32)
    rows = pair.shape[1]
    if not cube():
        return lax.psum_scatter(pair, "batch", scatter_dimension=0, tiled=True)[0]
    parts = [
        jnp.concatenate(
            [
                lax.dynamic_index_in_dim(pair, chip ^ offset, axis=0, keepdims=False)
                for offset in block_order(level)
            ]
        ).astype(jnp.bfloat16)
        for level in LEVELS
    ]
    return reduce_rows(parts, rows)


def decoupled_adam_step(master, first, second, grad, rate, decay):
    first_new = BETA_ONE * first + (1.0 - BETA_ONE) * grad
    second_new = BETA_TWO * second + (1.0 - BETA_TWO) * grad * grad
    first_hat = first_new / (1.0 - BETA_ONE**STEP)
    second_hat = second_new / (1.0 - BETA_TWO**STEP)
    master_new = master - rate * (first_hat / (jnp.sqrt(second_hat) + EPSILON) + decay * master)
    return (master_new, first_new, second_new)


def local(
    crop_maps,
    cotangent,
    crop_counts,
    filter_weight,
    filter_first,
    filter_second,
    conv_filter_bias,
    conv_filter_bias_mean,
    conv_filter_bias_variance,
    pool_stitch,
    pool_stitch_first,
    pool_stitch_second,
    dense_weight,
    dense_weight_first,
    dense_weight_second,
    dense_bias,
    dense_bias_first,
    dense_bias_second,
    dense_stitch,
    dense_stitch_first,
    dense_stitch_second,
):
    block_rows = crop_maps.shape[0]
    side = crop_maps.shape[2]
    in_width = crop_maps.shape[4]
    filter_rows, out_width = filter_weight.shape
    chips = lax.axis_size("batch")
    chip = lax.axis_index("batch")
    core = lax.axis_index("tower")
    totals = jnp.sum(crop_counts.reshape(2, -1), axis=1)
    slots = jnp.arange(block_rows, dtype=jnp.int32)
    mask = (slots[None, :] < totals[:, None]).astype(jnp.float32).reshape(-1)
    pair_rows = 2 * block_rows
    dense_rows, unit_width = dense_weight.shape[1:]
    half_width = unit_width // 2
    bias_width = conv_filter_bias.shape[0]
    small_width = bias_width + pool_stitch.shape[0]
    pack_rows = -(-(filter_rows + 1) // 16) * 16
    small = jnp.concatenate([conv_filter_bias, pool_stitch])
    small = jnp.pad(small, (0, (pack_rows - filter_rows) * out_width - small_width))
    packed = jnp.concatenate([filter_weight, small.reshape(-1, out_width)]).astype(jnp.bfloat16)
    gathered = gather_packed(packed)
    filters = gathered[:, :filter_rows].reshape(2, 3, 3, in_width, out_width)
    small_full = gathered[:, filter_rows, :small_width].astype(jnp.float32)
    biases = small_full[:, :bias_width].reshape(2, out_width)
    pool_low = small_full[:, bias_width:].reshape(2, 2, out_width)
    maps = jnp.transpose(crop_maps, (1, 2, 3, 0, 4))
    grad_out = cotangent.astype(jnp.float32) * mask[:, None, None]
    own_stitch = lax.dynamic_index_in_dim(dense_stitch, core, axis=1, keepdims=False)
    other_stitch = lax.dynamic_index_in_dim(dense_stitch, 1 - core, axis=1, keepdims=False)
    own_grad = jnp.sum(own_stitch * grad_out, axis=1).astype(jnp.bfloat16)
    other_grad = core_swap(jnp.sum(other_stitch * grad_out, axis=1).astype(jnp.bfloat16))
    grad_active = by_core(core, own_grad, other_grad)
    dense_low = dense_weight[0].astype(jnp.bfloat16)
    conv = jnp.stack(
        [
            lax.conv_general_dilated(
                maps[tower],
                filters[tower],
                (1, 1),
                ((1, 1), (1, 1)),
                dimension_numbers=("HWNC", "HWIO", "HWNC"),
                preferred_element_type=jnp.float32,
            )
            for tower in range(2)
        ]
    )
    conv = conv + biases[:, None, None, None, :]
    pooled = pool_mean(smooth_gate(conv))
    pooled_side = pooled.shape[1]
    mixed = jnp.sum(pool_low[:, :, None, None, None, :] * pooled[None], axis=1).astype(jnp.bfloat16)
    mixed = jnp.transpose(mixed, (0, 3, 1, 2, 4)).reshape(2, block_rows, chips, dense_rows)
    mixed = jnp.transpose(mixed, (0, 2, 1, 3))
    own_mixed = lax.dynamic_index_in_dim(mixed, core, axis=0, keepdims=False)
    other_mixed = core_swap(lax.dynamic_index_in_dim(mixed, 1 - core, axis=0, keepdims=False))
    features = jnp.where(
        core == 0,
        jnp.concatenate([own_mixed, other_mixed], axis=1),
        jnp.concatenate([other_mixed, own_mixed], axis=1),
    )
    columns = scatter_chunks(features, chip)
    partial = [
        jnp.dot(part, dense_low, preferred_element_type=jnp.float32).astype(jnp.bfloat16)
        for part in columns
    ]
    hidden = reduce_rows(partial, pair_rows) + dense_bias
    grad_hidden = (grad_active.astype(jnp.float32) * gate_slope(hidden)).astype(jnp.bfloat16)
    grad_full = gather_rows(grad_hidden)
    active = smooth_gate(hidden).astype(jnp.bfloat16)
    own_active = lax.dynamic_slice_in_dim(active, core * half_width, half_width, axis=1)
    other_active = core_swap(
        lax.dynamic_slice_in_dim(active, (1 - core) * half_width, half_width, axis=1)
    )
    own_active = own_active.astype(jnp.float32)[:, None]
    other_active = other_active.astype(jnp.float32)[:, None]
    stitched = own_stitch * own_active + other_stitch * other_active
    stitched = (stitched * mask[:, None, None]).astype(jnp.bfloat16)
    grad_own_stitch = jnp.sum(grad_out * own_active, axis=0)
    grad_other_stitch = jnp.sum(grad_out * other_active, axis=0)
    grad_dense_stitch = sum_batch(
        jnp.where(
            core == 0,
            jnp.stack([grad_own_stitch, grad_other_stitch], axis=1),
            jnp.stack([grad_other_stitch, grad_own_stitch], axis=1),
        )
    )
    grad_columns = [
        lax.dot_general(
            part, dense_low, (((1,), (1,)), ((), ())), preferred_element_type=jnp.float32
        ).astype(jnp.bfloat16)
        for part in grad_full
    ]
    returned = return_chunks(grad_columns, chip, pair_rows)
    columns = jnp.concatenate(columns)
    grad_full = jnp.concatenate(grad_full)
    grad_dense_bias = jnp.sum(grad_full.astype(jnp.float32), axis=0)
    grad_dense_weight = lax.dot_general(
        columns, grad_full, (((0,), (0,)), ((), ())), preferred_element_type=jnp.float32
    )
    halves = returned.reshape(chips, 2, block_rows, dense_rows)
    own_mixed = lax.dynamic_index_in_dim(halves, core, axis=1, keepdims=False)
    other_mixed = core_swap(lax.dynamic_index_in_dim(halves, 1 - core, axis=1, keepdims=False))
    grad_mixed = jnp.where(
        core == 0, jnp.stack([own_mixed, other_mixed]), jnp.stack([other_mixed, own_mixed])
    )
    grad_mixed = jnp.transpose(grad_mixed, (0, 2, 1, 3)).reshape(
        2, block_rows, pooled_side, pooled_side, out_width
    )
    grad_mixed = jnp.transpose(grad_mixed, (0, 2, 3, 1, 4)).astype(jnp.float32)
    grad_pool_stitch = jnp.sum(grad_mixed[:, None] * pooled[None], axis=(2, 3, 4))
    grad_pooled = jnp.sum(pool_low[:, :, None, None, None, :] * grad_mixed[:, None], axis=0)
    grad_conv = (pool_spread(grad_pooled, side) * gate_slope(conv)).astype(jnp.bfloat16)
    grad_filter_bias = jnp.sum(grad_conv.astype(jnp.float32), axis=(1, 2, 3))
    weight_dims = lax.ConvDimensionNumbers((3, 2, 0, 1), (3, 2, 0, 1), (2, 3, 0, 1))
    grad_filter_weight = jnp.stack(
        [
            lax.conv_general_dilated(
                maps[tower],
                grad_conv[tower],
                (1, 1),
                ((1, 1), (1, 1)),
                dimension_numbers=weight_dims,
                preferred_element_type=jnp.float32,
            ).astype(jnp.bfloat16)
            for tower in range(2)
        ]
    )
    filter_sums = reduce_filters(
        grad_filter_weight.reshape(chips, 2, filter_rows, out_width), chip, core
    )
    small_grad = jnp.concatenate(
        [grad_filter_bias.reshape(2 * chips, -1), grad_pool_stitch.reshape(2 * chips, -1)], axis=1
    )
    small_grad = sum_batch(small_grad + core_swap(small_grad))
    small_grad = lax.dynamic_index_in_dim(small_grad, chip * 2 + core, axis=0, keepdims=False)
    filter_bias_sums = small_grad[:bias_width]
    pool_sums = small_grad[bias_width:]
    input_grad = jnp.stack(
        [
            lax.conv_general_dilated(
                grad_conv[tower],
                filters[tower][::-1, ::-1],
                (1, 1),
                ((1, 1), (1, 1)),
                dimension_numbers=("HWNC", "HWOI", "HWNC"),
                preferred_element_type=jnp.float32,
            ).astype(jnp.bfloat16)
            for tower in range(2)
        ]
    )
    input_grad = jnp.transpose(input_grad, (3, 0, 1, 2, 4))
    updated_conv_weight, updated_conv_weight_mean, updated_conv_weight_variance = (
        decoupled_adam_step(
            filter_weight, filter_first, filter_second, filter_sums, RATE_FILTER, DECAY
        )
    )
    updated_conv_bias, updated_conv_bias_mean, updated_conv_bias_variance = decoupled_adam_step(
        conv_filter_bias,
        conv_filter_bias_mean,
        conv_filter_bias_variance,
        filter_bias_sums,
        BIAS_LEARN_RATE,
        0.0,
    )
    updated_pooling_stitch, updated_pooling_stitch_mean, updated_pooling_stitch_variance = (
        decoupled_adam_step(
            pool_stitch, pool_stitch_first, pool_stitch_second, pool_sums, RATE_STITCH, 0.0
        )
    )
    updated_dense_weight, updated_dense_weight_mean, updated_dense_weight_variance = (
        decoupled_adam_step(
            dense_weight,
            dense_weight_first,
            dense_weight_second,
            grad_dense_weight[None],
            RATE_DENSE,
            DECAY,
        )
    )
    updated_dense_bias, updated_dense_bias_mean, updated_dense_bias_variance = decoupled_adam_step(
        dense_bias, dense_bias_first, dense_bias_second, grad_dense_bias[None], BIAS_LEARN_RATE, 0.0
    )
    updated_dense_stitch, updated_dense_stitch_mean, updated_dense_stitch_variance = (
        decoupled_adam_step(
            dense_stitch,
            dense_stitch_first,
            dense_stitch_second,
            grad_dense_stitch,
            RATE_STITCH,
            0.0,
        )
    )
    return (
        stitched,
        input_grad,
        updated_conv_weight,
        updated_conv_weight_mean,
        updated_conv_weight_variance,
        updated_conv_weight.astype(jnp.bfloat16),
        updated_conv_bias,
        updated_conv_bias_mean,
        updated_conv_bias_variance,
        updated_pooling_stitch,
        updated_pooling_stitch_mean,
        updated_pooling_stitch_variance,
        updated_dense_weight,
        updated_dense_weight_mean,
        updated_dense_weight_variance,
        updated_dense_weight.astype(jnp.bfloat16),
        updated_dense_bias,
        updated_dense_bias_mean,
        updated_dense_bias_variance,
        updated_dense_stitch,
        updated_dense_stitch_mean,
        updated_dense_stitch_variance,
    )


def solution(mesh):
    in_specs = (
        P(("batch", "tower"), None, None, None, None),
        P("batch", None, "tower"),
        P("batch"),
        P(("batch", "tower"), None),
        P(("batch", "tower"), None),
        P(("batch", "tower"), None),
        P(("batch", "tower")),
        P(("batch", "tower")),
        P(("batch", "tower")),
        P(("batch", "tower")),
        P(("batch", "tower")),
        P(("batch", "tower")),
        P("tower", "batch", None),
        P("tower", "batch", None),
        P("tower", "batch", None),
        P("tower", None),
        P("tower", None),
        P("tower", None),
        P(None, None, "tower"),
        P(None, None, "tower"),
        P(None, None, "tower"),
    )
    out_specs = (
        P("batch", None, "tower"),
        P(("batch", "tower"), None, None, None, None),
        P(("batch", "tower"), None),
        P(("batch", "tower"), None),
        P(("batch", "tower"), None),
        P(("batch", "tower"), None),
        P(("batch", "tower")),
        P(("batch", "tower")),
        P(("batch", "tower")),
        P(("batch", "tower")),
        P(("batch", "tower")),
        P(("batch", "tower")),
        P("tower", "batch", None),
        P("tower", "batch", None),
        P("tower", "batch", None),
        P("tower", "batch", None),
        P("tower", None),
        P("tower", None),
        P("tower", None),
        P(None, None, "tower"),
        P(None, None, "tower"),
        P(None, None, "tower"),
    )
    return jax.shard_map(local, mesh=mesh, in_specs=in_specs, out_specs=out_specs, check_vma=False)
```

time: 3400 us -> 431 us (0.13)
  waiting for transfers between devices: 2610 us -> 75.6 us
  blocking collectives: 181 us -> 0 us
  local copies, waits for them, and re-layouts: 257 us -> 88.4 us
  matrix products: 229 us -> 84.4 us
  starting transfers between devices: 0.16 us -> 130 us
  other arithmetic: 101 us -> 46.1 us
    reduce_scatter x2 -> x0, waiting for transfers between devices: 1930 us -> none  [the longest x1 1930 us: local(): lax.psum_scatter(jnp.einsum('nr,nu->ru', columns, grad_hidden, preferred_...]
    all_gather x2 -> x0, waiting for transfers between devices: 679 us -> none  [the longest x1 678 us: local(): lax.all_gather(dense_low, 'batch', axis=0, tiled=True)]
    pad x9 -> x0, local copies, waits for them, and re-layouts: 216 us -> none  [pool_spread(): lax.pad(scaled, jnp.float32(0), ((0, 0, 0), (0, 0, 0), (row_start, row_en...]
    dot_general x30 -> x9, matrix products: 229 us -> 46.5 us  [the longest x1 26.2 us: local(): lax.dot_general(columns, grad_full, (((0,), (0,)), ((), ())), preferred_e...]
    ppermute x0 -> x97, starting transfers between devices: none -> 130 us  [the longest x90 128 us: hop(): return lax.ppermute(values, 'batch', [(i, i ^ offset) for i in range(CUBE)])]
    unnamed x2 -> x0, blocking collectives: 83.8 us -> none
    psum x1 -> x0, blocking collectives: 79.6 us -> none  [local(): lax.psum((grad_dense_stitch, grad_dense_bias), 'batch')]
    ppermute x0 -> x97, waiting for transfers between devices: none -> 75.6 us  [the longest x90 72.4 us: hop(): return lax.ppermute(values, 'batch', [(i, i ^ offset) for i in range(CUBE)])]
  transfers between devices with their start and end apart: 4 -> 97, of which waited for: 3 -> 33; matrix products, arithmetic and copies ran while one was open for 7% -> 32% of each run, Pallas kernels for 0% -> 0%
where the time goes in v1:
time: 431 us; the launch traced here: 427 us
  starting transfers between devices  130 us (30%)
  local copies, waits for them, and re-layouts  88.4 us (21%)
  matrix products  84.4 us (20%)
  waiting for transfers between devices  75.6 us (18%)
  other arithmetic  46.1 us (11%)
    ppermute x90, starting transfers between devices, hop(): return lax.ppermute(values, 'batch', [(i, i ^ offset) for i in range(CUBE)])  128 us
    ppermute x90, waiting for transfers between devices, hop(): return lax.ppermute(values, 'batch', [(i, i ^ offset) for i in range(CUBE)])  72.4 us
    unnamed x167, local copies, waits for them, and re-layouts  43.1 us
    dot_general x1, matrix products, local(): lax.dot_general(columns, grad_full, (((0,), (0,)), ((), ())), preferred_e...  26.2 us
    broadcast_in_dim x16, local copies, waits for them, and re-layouts, return_chunks(): block[None]  16.3 us
    conv_general_dilated x2, matrix products, local(): lax.conv_general_dilated(grad_conv[tower], filters[tower][::-1, ::-1], (1...  14.1 us
    conv_general_dilated x2, matrix products, local(): lax.conv_general_dilated(maps[tower], filters[tower], (1, 1), ((1, 1), (1...  13 us
    dot_general x4, matrix products, local(): lax.dot_general(part, dense_low, (((1,), (1,)), ((), ())), preferred_elem...  12.9 us
  transfers between devices with their start and end apart: 97, of which 33 were waited for; matrix products, arithmetic and copies ran while one was open for 32% of the time, Pallas kernels for 0%

profile of v1, /device:TPU:0, one launch (start us, length us, event | category | flops | bytes accessed | tf_op | source)
XLA Modules:
  0.0 426.9 jit_solution(14328799694307427677)
XLA Ops:
  2.4 3.0 collective-permute-start
  8.5 2.6 collective-permute-start.7
  15.3 4.3 %collective-permute-done.7 = bf16[224,256]{1,0:T(8,128)(2,1)S(1)} collective-permute-done((bf16[224,256]{1,0:T(8,128)(2,1)S(1)}, bf16[224,256]{1,0:T(8,128)(2,1)S(1)}, u32[]{:S(2)}, u32[]{:S(2)}) %collective-permute-start.7) | collective-permute-done | bytes 114720 | tf_op jit(solution)/shard_map/ppermute | solution.py:57
  31.2 4.7 %copy.228 = bf16[16,2,13,13,384]{4,0,3,2,1:T(8,128)(2,1)} copy(bf16[16,2,13,13,384]{4,1,3,2,0:T(2,128)(2,1)} %param.21) | data formatting | bytes 8306688 | tf_op args[0]
  35.9 2.7 maximum_select_fusion
  39.2 3.1 copy-done.4
  42.4 5.8 %fusion.28 = f32[1,13,13,16,256]{4,3,2,1,0:T(8,128)S(1)} fusion(bf16[3,3,384,256]{3,2,1,0:T(8,128)(2,1)S(1)} %bitcast.294, bf16[2,13,13,16,384]{4,3,2,1,0:T(8,128)(2,1)S(1)} %bitcast.286), kind=kOutput, calls=%fused_computation.57 | convolution fusion | flops 4306501632 | bytes 6615040 | tf_op jit(solution)/shard_map/conv_general_dilated | solution.py:254
  48.2 7.1 %fusion.29 = f32[1,13,13,16,256]{4,3,2,1,0:T(8,128)} fusion(bf16[3,3,384,256]{3,2,1,0:T(8,128)(2,1)S(1)} %bitcast.292, bf16[2,13,13,16,384]{4,3,2,1,0:T(8,128)(2,1)S(1)} %bitcast.287), kind=kOutput, calls=%fused_computation.58 | convolution fusion | flops 4306501632 | bytes 6615040 | tf_op jit(solution)/shard_map/conv_general_dilated | solution.py:254
  55.5 3.2 multiply_multiply_fusion.3
  58.7 1.7 add_multiply_fusion
  63.1 3.0 reshape.172
  69.3 2.4 constant_dynamic-slice_fusion.5
  72.3 2.7 collective-permute-start.17
  77.0 6.6 %convert_element_type.262 = bf16[1,576,4096]{2,1,0:T(8,128)(2,1)} convert(f32[1,576,4096]{2,1,0:T(8,128)} %param.33) | non-fusion elementwise | flops 2359296 | bytes 14155776 | tf_op jit(solution)/shard_map/convert_element_type | solution.py:251
  86.6 2.5 collective-permute-start.18
  90.0 2.5 collective-permute-start.19
  97.5 4.5 %collective-permute-start.25 = (bf16[32,576]{1,0:T(8,128)(2,1)S(1)}, bf16[32,576]{1,0:T(8,128)(2,1)S(1)}, u32[]{:S(2)}, u32[]{:S(2)}) collective-permute-start(bf16[32,576]{1,0:T(8,128)(2,1)S(1)} %bitcast.323), channel_id=1, source_target_pairs={{0,22},{2,20},{4,18},{6,16},{8,30},{10,28},{12,26},{14,24},{16,6},... | collective-permute-start | bytes 110600 | tf_op jit(solution)/shard_map/ppermute | solution.py:57
  102.1 3.2 collective-permute-start.27
  106.2 3.1 collective-permute-start.32
  109.6 2.9 collective-permute-start.34
  118.1 3.6 convolution_convert_fusion
  127.3 1.8 convolution_convert_fusion.3
  130.0 6.7 %collective-permute-done.41 = bf16[64,4096]{1,0:T(8,128)(2,1)S(1)} collective-permute-done((bf16[64,4096]{1,0:T(8,128)(2,1)S(1)}, bf16[64,4096]{1,0:T(8,128)(2,1)S(1)}, u32[]{:S(2)}, u32[]{:S(2)}) %collective-permute-start.41) | collective-permute-done | bytes 524320 | tf_op jit(solution)/shard_map/ppermute | solution.py:57
  140.1 7.8 %collective-permute-done.28 = bf16[64,4096]{1,0:T(8,128)(2,1)S(1)} collective-permute-done((bf16[64,4096]{1,0:T(8,128)(2,1)S(1)}, bf16[64,4096]{1,0:T(8,128)(2,1)S(1)}, u32[]{:S(2)}, u32[]{:S(2)}) %collective-permute-start.28) | collective-permute-done | bytes 524320 | tf_op jit(solution)/shard_map/ppermute | solution.py:57
  152.5 2.8 collective-permute-done.29
  155.4 2.8 collective-permute-start.30
  160.5 12.6 %collective-permute-done.30 = bf16[32,4096]{1,0:T(8,128)(2,1)S(1)} collective-permute-done((bf16[32,4096]{1,0:T(8,128)(2,1)S(1)}, bf16[32,4096]{1,0:T(8,128)(2,1)S(1)}, u32[]{:S(2)}, u32[]{:S(2)}) %collective-permute-start.30) | collective-permute-done | bytes 262176 | tf_op jit(solution)/shard_map/ppermute | solution.py:57
  177.0 3.4 multiply_reduce_fusion.4
  186.5 1.9 collective-permute-start.45
  192.7 3.4 collective-permute-start.95
  198.1 2.6 collective-permute-start.96
  201.1 2.0 collective-permute-start.61
  204.3 3.8 fusion.40
  223.6 3.3 collective-permute-done.74
  232.6 2.1 collective-permute-done.47
  234.8 4.1 fusion.31
  239.0 2.6 collective-permute-start.49
  248.4 3.2 collective-permute-start.50
  253.9 1.9 collective-permute-start.51
  259.2 1.8 collective-permute-start.52
  263.4 2.6 fusion.34
  270.4 26.2 %fusion.149 = (bf16[1,576,4096]{2,1,0:T(8,128)(2,1)}, f32[1,576,4096]{2,1,0:T(8,128)}, f32[1,576,4096]{2,1,0:T(8,128)}, f32[1,576,4096]{2,1,0:T(8,128)}) fusion(f32[1,576,4096]{2,1,0:T(8,128)} %param.33, f32[1,576,4096]{2,1,0:T(8,128)} %param.34, f32[1,576,4096]{2,1,0:T(8,128)} %param.35, bf16[512,576]{1,0:T(8,128)(2,1)} %constant_dynamic-update-slice_fusion, ...), kind=kOutput, calls=%fused_computation.368 | convolution fusion | flops 2451308544 | bytes 66125824 | tf_op jit(solution)/shard_map/dot_general | solution.py:314
  296.6 2.5 fusion.37
  299.1 4.6 %collective-permute-start.58 = (bf16[32,576]{0,1:T(8,128)(2,1)S(1)}, bf16[32,576]{0,1:T(8,128)(2,1)S(1)}, u32[]{:S(2)}, u32[]{:S(2)}) collective-permute-start(bf16[32,576]{0,1:T(8,128)(2,1)S(1)} %get-tuple-element.219), channel_id=1, source_target_pairs={{0,22},{2,20},{4,18},{6,16},{8,30},{10,28},{12,26},{14,24},{16,6},... | collective-permute-start | bytes 110600 | tf_op jit(solution)/shard_map/ppermute | solution.py:57
  304.6 3.1 collective-permute-start.60
  308.0 3.8 collective-permute-start.66
  311.7 2.3 collective-permute-done.58
  314.1 4.2 collective-permute-done.59
  318.3 3.2 convert_reduce_fusion
  337.9 3.0 reshape.183
  340.8 2.2 copy.168
  349.1 4.6 %convert_reduce_fusion.1 = (f32[2,256]{1,0:T(2,128)}, bf16[2,13,13,16,256]{4,3,2,1,0:T(8,128)(2,1)S(1)}) fusion(f32[2,256]{1,0:T(2,128)S(1)} %copy-done.45, f32[1,13,13,16,256]{4,3,2,1,0:T(8,128)S(1)} %fusion.28, f32[1,13,13,16,256]{4,3,2,1,0:T(8,128)S(1)} %copy-done.2, f32[2,13,14,16,256]{4,3,2,1,0:T(8,128)S(1)} %bitcast.278), kind=kLoop, calls=%fused_computation.19 | loop fusion | flops 31841792 | bytes 13848576 | tf_op jit(solution)/shard_map/reduce_sum | solution.py:330
  353.7 5.4 %convert_bitcast_fusion.2 = bf16[1,3,3,384,256]{4,3,2,1,0:T(8,128)(2,1)S(1)} fusion(bf16[2,13,13,16,384]{4,3,2,1,0:T(8,128)(2,1)S(1)} %bitcast.288, bf16[2,13,13,16,256]{4,3,2,1,0:T(8,128)(2,1)S(1)} %get-tuple-element.157), kind=kOutput, calls=%fused_computation.60 | convolution fusion | flops 4307386368 | bytes 5230592 | tf_op jit(solution)/shard_map/conv_general_dilated | solution.py:334
  359.1 5.4 %convert_bitcast_fusion.3 = bf16[1,3,3,384,256]{4,3,2,1,0:T(8,128)(2,1)S(1)} fusion(bf16[2,13,13,16,384]{4,3,2,1,0:T(8,128)(2,1)S(1)} %bitcast.289, bf16[2,13,13,16,256]{4,3,2,1,0:T(8,128)(2,1)S(1)} %get-tuple-element.157), kind=kOutput, calls=%fused_computation.61 | convolution fusion | flops 4307386368 | bytes 5230592 | tf_op jit(solution)/shard_map/conv_general_dilated | solution.py:334
  370.5 2.0 collective-permute-done.89
  373.4 7.0 %convert_bitcast_fusion = bf16[1,13,13,16,384]{4,3,2,1,0:T(8,128)(2,1)S(1)} fusion(bf16[3,3,384,256]{3,2,1,0:T(8,128)(2,1)S(1)} %bitcast.295, bf16[2,13,13,16,256]{4,3,2,1,0:T(8,128)(2,1)S(1)} %copy-done.7), kind=kOutput, calls=%fused_computation.51 | convolution fusion | flops 4307539968 | bytes 5230592 | tf_op jit(solution)/shard_map/conv_general_dilated | solution.py:357
  380.5 2.4 collective-permute-start.91
  383.0 7.1 %convert_bitcast_fusion.1 = bf16[1,13,13,16,384]{4,3,2,1,0:T(8,128)(2,1)S(1)} fusion(bf16[3,3,384,256]{3,2,1,0:T(8,128)(2,1)S(1)} %bitcast.293, bf16[2,13,13,16,256]{4,3,2,1,0:T(8,128)(2,1)S(1)} %copy-done.7), kind=kOutput, calls=%fused_computation.52 | convolution fusion | flops 4307539968 | bytes 5230592 | tf_op jit(solution)/shard_map/conv_general_dilated | solution.py:357
  391.7 5.2 %copy.176 = bf16[16,2,13,13,384]{4,1,3,2,0:T(2,128)(2,1)} copy(bf16[16,2,13,13,384]{4,0,3,2,1:T(8,128)(2,1)S(1)} %maximum_bitcast_fusion) | data formatting | bytes 8306688
  397.4 1.9 convert_add_fusion
  404.0 4.0 collective-permute-done.86
  416.3 1.9 collective-permute-start.82
  418.4 2.2 collective-permute-start.79
  421.1 4.5 %collective-permute-done.82 = bf16[216,256]{1,0:T(8,128)(2,1)S(1)} collective-permute-done((bf16[216,256]{1,0:T(8,128)(2,1)S(1)}, bf16[216,256]{1,0:T(8,128)(2,1)S(1)}, u32[]{:S(2)}, u32[]{:S(2)}) %collective-permute-start.82) | collective-permute-done | bytes 110624 | tf_op jit(solution)/shard_map/ppermute | solution.py:57
  (469 shorter events, 167.2 us)
Async XLA Ops:
  2.4 10.2 %collective-permute-start = (bf16[224,256]{1,0:T(8,128)(2,1)S(1)}, bf16[224,256]{1,0:T(8,128)(2,1)S(1)}, u32[]{:S(2)}, u32[]{:S(2)}) collective-permute-start(bf16[224,256]{1,0:T(8,128)(2,1)S(1)} %pad_maximum_fusion.7), channel_id=1, source_target_pairs={{0,2},{2,0},{4,6},{6,4},{8,10},{10,8},{12,14},{14,12},{16,18},{18,... | collective-permute-start | bytes 344072 | tf_op jit(solution)/shard_map/ppermute | solution.py:57
  5.4 9.3 %collective-permute-start.1 = (bf16[224,256]{1,0:T(8,128)(2,1)S(1)}, bf16[224,256]{1,0:T(8,128)(2,1)S(1)}, u32[]{:S(2)}, u32[]{:S(2)}) collective-permute-start(bf16[224,256]{1,0:T(8,128)(2,1)S(1)} %pad_maximum_fusion.7), channel_id=1, source_target_pairs={{0,4},{2,6},{4,0},{6,2},{8,12},{10,14},{12,8},{14,10},{16,20},{18,... | collective-permute-start | bytes 344072 | tf_op jit(solution)/shard_map/ppermute | solution.py:57
  8.5 11.1 %collective-permute-start.7 = (bf16[224,256]{1,0:T(8,128)(2,1)S(1)}, bf16[224,256]{1,0:T(8,128)(2,1)S(1)}, u32[]{:S(2)}, u32[]{:S(2)}) collective-permute-start(bf16[224,256]{1,0:T(8,128)(2,1)S(1)} %pad_maximum_fusion.7), channel_id=1, source_target_pairs={{0,16},{2,18},{4,20},{6,22},{8,24},{10,26},{12,28},{14,30},{16,0},... | collective-permute-start | bytes 344072 | tf_op jit(solution)/shard_map/ppermute | solution.py:57
  11.1 9.1 %collective-permute-start.11 = (bf16[224,256]{1,0:T(8,128)(2,1)S(1)}, bf16[224,256]{1,0:T(8,128)(2,1)S(1)}, u32[]{:S(2)}, u32[]{:S(2)}) collective-permute-start(bf16[224,256]{1,0:T(8,128)(2,1)S(1)} %pad_maximum_fusion.7), channel_id=1, source_target_pairs={{0,24},{2,26},{4,28},{6,30},{8,16},{10,18},{12,20},{14,22},{16,8},... | collective-permute-start | bytes 344072 | tf_op jit(solution)/shard_map/ppermute | solution.py:57
  12.6 8.2 %collective-permute-start.2 = (bf16[224,256]{1,0:T(8,128)(2,1)S(1)}, bf16[224,256]{1,0:T(8,128)(2,1)S(1)}, u32[]{:S(2)}, u32[]{:S(2)}) collective-permute-start(bf16[224,256]{1,0:T(8,128)(2,1)S(1)} %collective-permute-done), channel_id=1, source_target_pairs={{0,4},{2,6},{4,0},{6,2},{8,12},{10,14},{12,8},{14,10},{16,20},{18,... | collective-permute-start | bytes 344072 | tf_op jit(solution)/shard_map/ppermute | solution.py:57
  13.1 9.2 %collective-permute-start.4 = (bf16[224,256]{1,0:T(8,128)(2,1)S(1)}, bf16[224,256]{1,0:T(8,128)(2,1)S(1)}, u32[]{:S(2)}, u32[]{:S(2)}) collective-permute-start(bf16[224,256]{1,0:T(8,128)(2,1)S(1)} %collective-permute-done.3), channel_id=1, source_target_pairs={{0,4},{2,6},{4,0},{6,2},{8,12},{10,14},{12,8},{14,10},{16,20},{18,... | collective-permute-start | bytes 344072 | tf_op jit(solution)/shard_map/ppermute | solution.py:57
  14.7 9.2 %collective-permute-start.5 = (bf16[224,256]{1,0:T(8,128)(2,1)S(1)}, bf16[224,256]{1,0:T(8,128)(2,1)S(1)}, u32[]{:S(2)}, u32[]{:S(2)}) collective-permute-start(bf16[224,256]{1,0:T(8,128)(2,1)S(1)} %collective-permute-done.3), channel_id=1, source_target_pairs={{0,2},{2,0},{4,6},{6,4},{8,10},{10,8},{12,14},{14,12},{16,18},{18,... | collective-permute-start | bytes 344072 | tf_op jit(solution)/shard_map/ppermute | solution.py:57
  20.2 8.6 %collective-permute-start.9 = (bf16[224,256]{1,0:T(8,128)(2,1)S(1)}, bf16[224,256]{1,0:T(8,128)(2,1)S(1)}, u32[]{:S(2)}, u32[]{:S(2)}) collective-permute-start(bf16[224,256]{1,0:T(8,128)(2,1)S(1)} %collective-permute-done.7), channel_id=1, source_target_pairs={{0,4},{2,6},{4,0},{6,2},{8,12},{10,14},{12,8},{14,10},{16,20},{18,... | collective-permute-start | bytes 344072 | tf_op jit(solution)/shard_map/ppermute | solution.py:57
  72.3 24.3 %collective-permute-start.17 = (bf16[32,576]{1,0:T(8,128)(2,1)}, bf16[32,576]{1,0:T(8,128)(2,1)}, u32[]{:S(2)}, u32[]{:S(2)}) collective-permute-start(bf16[32,576]{1,0:T(8,128)(2,1)} %bitcast.274), channel_id=1, source_target_pairs={{0,28},{2,30},{4,24},{6,26},{8,20},{10,22},{12,16},{14,18},{16,12}... | collective-permute-start | bytes 110600 | tf_op jit(solution)/shard_map/ppermute | solution.py:57
  84.5 33.5 %collective-permute-start.40 = (bf16[32,576]{1,0:T(8,128)(2,1)S(1)}, bf16[32,576]{1,0:T(8,128)(2,1)S(1)}, u32[]{:S(2)}, u32[]{:S(2)}) collective-permute-start(bf16[32,576]{1,0:T(8,128)(2,1)S(1)} %bitcast.314), channel_id=1, source_target_pairs={{0,4},{2,6},{4,0},{6,2},{8,12},{10,14},{12,8},{14,10},{16,20},{18,... | collective-permute-start | bytes 110600 | tf_op jit(solution)/shard_map/ppermute | solution.py:57
  86.6 10.9 %collective-permute-start.18 = (bf16[32,576]{1,0:T(8,128)(2,1)S(1)}, bf16[32,576]{1,0:T(8,128)(2,1)S(1)}, u32[]{:S(2)}, u32[]{:S(2)}) collective-permute-start(bf16[32,576]{1,0:T(8,128)(2,1)S(1)} %bitcast.327), channel_id=1, source_target_pairs={{0,30},{2,28},{4,26},{6,24},{8,22},{10,20},{12,18},{14,16},{16,14}... | collective-permute-start | bytes 110600 | tf_op jit(solution)/shard_map/ppermute | solution.py:57
  90.0 12.0 %collective-permute-start.19 = (bf16[32,576]{1,0:T(8,128)(2,1)S(1)}, bf16[32,576]{1,0:T(8,128)(2,1)S(1)}, u32[]{:S(2)}, u32[]{:S(2)}) collective-permute-start(bf16[32,576]{1,0:T(8,128)(2,1)S(1)} %bitcast.326), channel_id=1, source_target_pairs={{0,24},{2,26},{4,28},{6,30},{8,16},{10,18},{12,20},{14,22},{16,8},... | collective-permute-start | bytes 110600 | tf_op jit(solution)/shard_map/ppermute | solution.py:57
  93.4 8.7 %collective-permute-start.20 = (bf16[32,576]{1,0:T(8,128)(2,1)S(1)}, bf16[32,576]{1,0:T(8,128)(2,1)S(1)}, u32[]{:S(2)}, u32[]{:S(2)}) collective-permute-start(bf16[32,576]{1,0:T(8,128)(2,1)S(1)} %bitcast.325), channel_id=1, source_target_pairs={{0,26},{2,24},{4,30},{6,28},{8,18},{10,16},{12,22},{14,20},{16,10}... | collective-permute-start | bytes 110600 | tf_op jit(solution)/shard_map/ppermute | solution.py:57
  96.7 8.7 %collective-permute-start.24 = (bf16[32,576]{1,0:T(8,128)(2,1)S(1)}, bf16[32,576]{1,0:T(8,128)(2,1)S(1)}, u32[]{:S(2)}, u32[]{:S(2)}) collective-permute-start(bf16[32,576]{1,0:T(8,128)(2,1)S(1)} %bitcast.324), channel_id=1, source_target_pairs={{0,18},{2,16},{4,22},{6,20},{8,26},{10,24},{12,30},{14,28},{16,2},... | collective-permute-start | bytes 110600 | tf_op jit(solution)/shard_map/ppermute | solution.py:57
  97.5 8.7 %collective-permute-start.25 = (bf16[32,576]{1,0:T(8,128)(2,1)S(1)}, bf16[32,576]{1,0:T(8,128)(2,1)S(1)}, u32[]{:S(2)}, u32[]{:S(2)}) collective-permute-start(bf16[32,576]{1,0:T(8,128)(2,1)S(1)} %bitcast.323), channel_id=1, source_target_pairs={{0,22},{2,20},{4,18},{6,16},{8,30},{10,28},{12,26},{14,24},{16,6},... | collective-permute-start | bytes 110600 | tf_op jit(solution)/shard_map/ppermute | solution.py:57
  121.8 14.9 %collective-permute-start.41 = (bf16[64,4096]{1,0:T(8,128)(2,1)S(1)}, bf16[64,4096]{1,0:T(8,128)(2,1)S(1)}, u32[]{:S(2)}, u32[]{:S(2)}) collective-permute-start(bf16[64,4096]{1,0:T(8,128)(2,1)S(1)} %slice.311), channel_id=1, source_target_pairs={{0,2},{2,0},{4,6},{6,4},{8,10},{10,8},{12,14},{14,12},{16,18},{18,... | collective-permute-start | bytes 1572872 | tf_op jit(solution)/shard_map/ppermute | solution.py:57
  124.4 14.9 %collective-permute-start.35 = (bf16[64,4096]{1,0:T(8,128)(2,1)S(1)}, bf16[64,4096]{1,0:T(8,128)(2,1)S(1)}, u32[]{:S(2)}, u32[]{:S(2)}) collective-permute-start(bf16[64,4096]{1,0:T(8,128)(2,1)S(1)} %slice.307), channel_id=1, source_target_pairs={{0,4},{2,6},{4,0},{6,2},{8,12},{10,14},{12,8},{14,10},{16,20},{18,... | collective-permute-start | bytes 1572872 | tf_op jit(solution)/shard_map/ppermute | solution.py:57
  126.2 21.6 %collective-permute-start.28 = (bf16[64,4096]{1,0:T(8,128)(2,1)S(1)}, bf16[64,4096]{1,0:T(8,128)(2,1)S(1)}, u32[]{:S(2)}, u32[]{:S(2)}) collective-permute-start(bf16[64,4096]{1,0:T(8,128)(2,1)S(1)} %slice.303), channel_id=1, source_target_pairs={{0,2},{2,0},{4,6},{6,4},{8,10},{10,8},{12,14},{14,12},{16,18},{18,... | collective-permute-start | bytes 1572872 | tf_op jit(solution)/shard_map/ppermute | solution.py:57
  129.2 20.5 %collective-permute-start.21 = (bf16[64,4096]{1,0:T(8,128)(2,1)S(1)}, bf16[64,4096]{1,0:T(8,128)(2,1)S(1)}, u32[]{:S(2)}, u32[]{:S(2)}) collective-permute-start(bf16[64,4096]{1,0:T(8,128)(2,1)S(1)} %slice.299), channel_id=1, source_target_pairs={{0,4},{2,6},{4,0},{6,2},{8,12},{10,14},{12,8},{14,10},{16,20},{18,... | collective-permute-start | bytes 1572872 | tf_op jit(solution)/shard_map/ppermute | solution.py:57
  136.9 23.6 %collective-permute-start.42 = (bf16[32,4096]{1,0:T(8,128)(2,1)S(1)}, bf16[32,4096]{1,0:T(8,128)(2,1)S(1)}, u32[]{:S(2)}, u32[]{:S(2)}) collective-permute-start(bf16[32,4096]{1,0:T(8,128)(2,1)S(1)} %slice.420), channel_id=1, source_target_pairs={{0,4},{2,6},{4,0},{6,2},{8,12},{10,14},{12,8},{14,10},{16,20},{18,... | collective-permute-start | bytes 786440 | tf_op jit(solution)/shard_map/ppermute | solution.py:57
  139.5 11.4 %collective-permute-start.36 = (bf16[32,4096]{1,0:T(8,128)(2,1)S(1)}, bf16[32,4096]{1,0:T(8,128)(2,1)S(1)}, u32[]{:S(2)}, u32[]{:S(2)}) collective-permute-start(bf16[32,4096]{1,0:T(8,128)(2,1)S(1)} %slice.421), channel_id=1, source_target_pairs={{0,2},{2,0},{4,6},{6,4},{8,10},{10,8},{12,14},{14,12},{16,18},{18,... | collective-permute-start | bytes 786440 | tf_op jit(solution)/shard_map/ppermute | solution.py:57
  149.8 8.3 %collective-permute-start.22 = (bf16[32,4096]{1,0:T(8,128)(2,1)S(1)}, bf16[32,4096]{1,0:T(8,128)(2,1)S(1)}, u32[]{:S(2)}, u32[]{:S(2)}) collective-permute-start(bf16[32,4096]{1,0:T(8,128)(2,1)S(1)} %slice.423), channel_id=1, source_target_pairs={{0,2},{2,0},{4,6},{6,4},{8,10},{10,8},{12,14},{14,12},{16,18},{18,... | collective-permute-start | bytes 786440 | tf_op jit(solution)/shard_map/ppermute | solution.py:57
  151.0 9.5 %collective-permute-start.37 = (bf16[32,4096]{1,0:T(8,128)(2,1)S(1)}, bf16[32,4096]{1,0:T(8,128)(2,1)S(1)}, u32[]{:S(2)}, u32[]{:S(2)}) collective-permute-start(bf16[32,4096]{1,0:T(8,128)(2,1)S(1)} %fusion.81), channel_id=1, source_target_pairs={{0,8},{2,10},{4,12},{6,14},{8,0},{10,2},{12,4},{14,6},{16,24},{18,... | collective-permute-start | bytes 786440 | tf_op jit(solution)/shard_map/ppermute | solution.py:57
  155.4 17.7 %collective-permute-start.30 = (bf16[32,4096]{1,0:T(8,128)(2,1)S(1)}, bf16[32,4096]{1,0:T(8,128)(2,1)S(1)}, u32[]{:S(2)}, u32[]{:S(2)}) collective-permute-start(bf16[32,4096]{1,0:T(8,128)(2,1)S(1)} %fusion.82), channel_id=1, source_target_pairs={{0,16},{2,18},{4,20},{6,22},{8,24},{10,26},{12,28},{14,30},{16,0},... | collective-permute-start | bytes 786440 | tf_op jit(solution)/shard_map/ppermute | solution.py:57
  158.2 14.9 %collective-permute-start.23 = (bf16[32,4096]{1,0:T(8,128)(2,1)S(1)}, bf16[32,4096]{1,0:T(8,128)(2,1)S(1)}, u32[]{:S(2)}, u32[]{:S(2)}) collective-permute-start(bf16[32,4096]{1,0:T(8,128)(2,1)S(1)} %fusion.83), channel_id=1, source_target_pairs={{0,24},{2,26},{4,28},{6,30},{8,16},{10,18},{12,20},{14,22},{16,8},... | collective-permute-start | bytes 786440 | tf_op jit(solution)/shard_map/ppermute | solution.py:57
  182.4 8.6 %collective-permute-start.69 = (bf16[32,4096]{1,0:T(8,128)(2,1)S(1)}, bf16[32,4096]{1,0:T(8,128)(2,1)S(1)}, u32[]{:S(2)}, u32[]{:S(2)}) collective-permute-start(bf16[32,4096]{1,0:T(8,128)(2,1)S(1)} %fusion.78), channel_id=1, source_target_pairs={{0,2},{2,0},{4,6},{6,4},{8,10},{10,8},{12,14},{14,12},{16,18},{18,... | collective-permute-start | bytes 786440 | tf_op jit(solution)/shard_map/ppermute | solution.py:57
  186.5 14.6 %collective-permute-start.45 = (bf16[32,4096]{1,0:T(8,128)(2,1)S(1)}, bf16[32,4096]{1,0:T(8,128)(2,1)}, u32[]{:S(2)}, u32[]{:S(2)}) collective-permute-start(bf16[32,4096]{1,0:T(8,128)(2,1)S(1)} %fusion.78), channel_id=1, source_target_pairs={{0,24},{2,26},{4,28},{6,30},{8,16},{10,18},{12,20},{14,22},{16,8},... | collective-permute-start | bytes 786440 | tf_op jit(solution)/shard_map/ppermute | solution.py:57
  188.4 14.7 %collective-permute-start.71 = (bf16[32,4096]{1,0:T(8,128)(2,1)S(1)}, bf16[32,4096]{1,0:T(8,128)(2,1)S(1)}, u32[]{:S(2)}, u32[]{:S(2)}) collective-permute-start(bf16[32,4096]{1,0:T(8,128)(2,1)S(1)} %fusion.78), channel_id=1, source_target_pairs={{0,4},{2,6},{4,0},{6,2},{8,12},{10,14},{12,8},{14,10},{16,20},{18,... | collective-permute-start | bytes 786440 | tf_op jit(solution)/shard_map/ppermute | solution.py:57
  191.0 13.3 %collective-permute-start.70 = (bf16[32,4096]{1,0:T(8,128)(2,1)S(1)}, bf16[32,4096]{1,0:T(8,128)(2,1)S(1)}, u32[]{:S(2)}, u32[]{:S(2)}) collective-permute-start(bf16[32,4096]{1,0:T(8,128)(2,1)S(1)} %collective-permute-done.69), channel_id=1, source_target_pairs={{0,4},{2,6},{4,0},{6,2},{8,12},{10,14},{12,8},{14,10},{16,20},{18,... | collective-permute-start | bytes 786440 | tf_op jit(solution)/shard_map/ppermute | solution.py:57
  198.1 11.6 %collective-permute-start.96 = (f32[2,2,2048]{2,0,1:T(2,128)S(1)}, f32[2,2,2048]{2,0,1:T(2,128)S(1)}, u32[]{:S(2)}, u32[]{:S(2)}) collective-permute-start(f32[2,2,2048]{2,0,1:T(2,128)S(1)} %add.489), channel_id=1, source_target_pairs={{0,16},{2,18},{4,20},{6,22},{8,24},{10,26},{12,28},{14,30},{16,0},... | collective-permute-start | bytes 98312 | tf_op jit(solution)/shard_map/ppermute | solution.py:57
  200.7 13.3 %collective-permute-start.53 = (bf16[32,4096]{1,0:T(8,128)(2,1)S(1)}, bf16[32,4096]{1,0:T(8,128)(2,1)}, u32[]{:S(2)}, u32[]{:S(2)}) collective-permute-start(bf16[32,4096]{1,0:T(8,128)(2,1)S(1)} %fusion.78), channel_id=1, source_target_pairs={{0,16},{2,18},{4,20},{6,22},{8,24},{10,26},{12,28},{14,30},{16,0},... | collective-permute-start | bytes 786440 | tf_op jit(solution)/shard_map/ppermute | solution.py:57
  201.1 14.5 %collective-permute-start.61 = (bf16[32,4096]{1,0:T(8,128)(2,1)S(1)}, bf16[32,4096]{1,0:T(8,128)(2,1)}, u32[]{:S(2)}, u32[]{:S(2)}) collective-permute-start(bf16[32,4096]{1,0:T(8,128)(2,1)S(1)} %fusion.78), channel_id=1, source_target_pairs={{0,8},{2,10},{4,12},{6,14},{8,0},{10,2},{12,4},{14,6},{16,24},{18,... | collective-permute-start | bytes 786440 | tf_op jit(solution)/shard_map/ppermute | solution.py:57
  203.1 12.9 %collective-permute-start.46 = (bf16[32,4096]{1,0:T(8,128)(2,1)}, bf16[32,4096]{1,0:T(8,128)(2,1)}, u32[]{:S(2)}, u32[]{:S(2)}) collective-permute-start(bf16[32,4096]{1,0:T(8,128)(2,1)} %collective-permute-done.45), channel_id=1, source_target_pairs={{0,4},{2,6},{4,0},{6,2},{8,12},{10,14},{12,8},{14,10},{16,20},{18,... | collective-permute-start | bytes 786440 | tf_op jit(solution)/shard_map/ppermute | solution.py:57
  209.0 8.3 %collective-permute-start.72 = (bf16[32,576]{0,1:T(8,128)(2,1)S(1)}, bf16[32,576]{0,1:T(8,128)(2,1)S(1)}, u32[]{:S(2)}, u32[]{:S(2)}) collective-permute-start(bf16[32,576]{0,1:T(8,128)(2,1)S(1)} %get-tuple-element.212), channel_id=1, source_target_pairs={{0,2},{2,0},{4,6},{6,4},{8,10},{10,8},{12,14},{14,12},{16,18},{18,... | collective-permute-start | bytes 110600 | tf_op jit(solution)/shard_map/ppermute | solution.py:57
  209.7 8.4 %collective-permute-start.73 = (bf16[32,576]{0,1:T(8,128)(2,1)S(1)}, bf16[32,576]{0,1:T(8,128)(2,1)S(1)}, u32[]{:S(2)}, u32[]{:S(2)}) collective-permute-start(bf16[32,576]{0,1:T(8,128)(2,1)S(1)} %get-tuple-element.211), channel_id=1, source_target_pairs={{0,6},{2,4},{4,2},{6,0},{8,14},{10,12},{12,10},{14,8},{16,22},{18,... | collective-permute-start | bytes 110600 | tf_op jit(solution)/shard_map/ppermute | solution.py:57
  214.0 15.8 %collective-permute-start.48 = (bf16[32,4096]{1,0:T(8,128)(2,1)}, bf16[32,4096]{1,0:T(8,128)(2,1)}, u32[]{:S(2)}, u32[]{:S(2)}) collective-permute-start(bf16[32,4096]{1,0:T(8,128)(2,1)} %collective-permute-done.45), channel_id=1, source_target_pairs={{0,2},{2,0},{4,6},{6,4},{8,10},{10,8},{12,14},{14,12},{16,18},{18,... | collective-permute-start | bytes 786440 | tf_op jit(solution)/shard_map/ppermute | solution.py:57
  215.6 15.4 %collective-permute-start.54 = (bf16[32,4096]{1,0:T(8,128)(2,1)}, bf16[32,4096]{1,0:T(8,128)(2,1)}, u32[]{:S(2)}, u32[]{:S(2)}) collective-permute-start(bf16[32,4096]{1,0:T(8,128)(2,1)} %collective-permute-done.53), channel_id=1, source_target_pairs={{0,2},{2,0},{4,6},{6,4},{8,10},{10,8},{12,14},{14,12},{16,18},{18,... | collective-permute-start | bytes 786440 | tf_op jit(solution)/shard_map/ppermute | solution.py:57
  216.0 16.3 %collective-permute-start.62 = (bf16[32,4096]{1,0:T(8,128)(2,1)}, bf16[32,4096]{1,0:T(8,128)(2,1)}, u32[]{:S(2)}, u32[]{:S(2)}) collective-permute-start(bf16[32,4096]{1,0:T(8,128)(2,1)} %collective-permute-done.61), channel_id=1, source_target_pairs={{0,4},{2,6},{4,0},{6,2},{8,12},{10,14},{12,8},{14,10},{16,20},{18,... | collective-permute-start | bytes 786440 | tf_op jit(solution)/shard_map/ppermute | solution.py:57
  217.3 9.6 %collective-permute-start.74 = (bf16[32,576]{0,1:T(8,128)(2,1)}, bf16[32,576]{0,1:T(8,128)(2,1)}, u32[]{:S(2)}, u32[]{:S(2)}) collective-permute-start(bf16[32,576]{0,1:T(8,128)(2,1)} %get-tuple-element.209), channel_id=1, source_target_pairs={{0,4},{2,6},{4,0},{6,2},{8,12},{10,14},{12,8},{14,10},{16,20},{18,... | collective-permute-start | bytes 110600 | tf_op jit(solution)/shard_map/ppermute | solution.py:57
  218.1 16.7 %collective-permute-start.47 = (bf16[32,4096]{1,0:T(8,128)(2,1)}, bf16[32,4096]{1,0:T(8,128)(2,1)}, u32[]{:S(2)}, u32[]{:S(2)}) collective-permute-start(bf16[32,4096]{1,0:T(8,128)(2,1)} %collective-permute-done.46), channel_id=1, source_target_pairs={{0,2},{2,0},{4,6},{6,4},{8,10},{10,8},{12,14},{14,12},{16,18},{18,... | collective-permute-start | bytes 786440 | tf_op jit(solution)/shard_map/ppermute | solution.py:57
  226.9 27.0 %collective-permute-start.56 = (bf16[32,4096]{1,0:T(8,128)(2,1)}, bf16[32,4096]{1,0:T(8,128)(2,1)}, u32[]{:S(2)}, u32[]{:S(2)}) collective-permute-start(bf16[32,4096]{1,0:T(8,128)(2,1)} %collective-permute-done.53), channel_id=1, source_target_pairs={{0,4},{2,6},{4,0},{6,2},{8,12},{10,14},{12,8},{14,10},{16,20},{18,... | collective-permute-start | bytes 786440 | tf_op jit(solution)/shard_map/ppermute | solution.py:57
  229.8 37.0 %collective-permute-start.64 = (bf16[32,4096]{1,0:T(8,128)(2,1)}, bf16[32,4096]{1,0:T(8,128)(2,1)S(1)}, u32[]{:S(2)}, u32[]{:S(2)}) collective-permute-start(bf16[32,4096]{1,0:T(8,128)(2,1)} %collective-permute-done.61), channel_id=1, source_target_pairs={{0,2},{2,0},{4,6},{6,4},{8,10},{10,8},{12,14},{14,12},{16,18},{18,... | collective-permute-start | bytes 786440 | tf_op jit(solution)/shard_map/ppermute | solution.py:57
  231.0 17.3 %collective-permute-start.55 = (bf16[32,4096]{1,0:T(8,128)(2,1)}, bf16[32,4096]{1,0:T(8,128)(2,1)S(1)}, u32[]{:S(2)}, u32[]{:S(2)}) collective-permute-start(bf16[32,4096]{1,0:T(8,128)(2,1)} %collective-permute-done.54), channel_id=1, source_target_pairs={{0,4},{2,6},{4,0},{6,2},{8,12},{10,14},{12,8},{14,10},{16,20},{18,... | collective-permute-start | bytes 786440 | tf_op jit(solution)/shard_map/ppermute | solution.py:57
  232.3 26.9 %collective-permute-start.63 = (bf16[32,4096]{1,0:T(8,128)(2,1)}, bf16[32,4096]{1,0:T(8,128)(2,1)S(1)}, u32[]{:S(2)}, u32[]{:S(2)}) collective-permute-start(bf16[32,4096]{1,0:T(8,128)(2,1)} %collective-permute-done.62), channel_id=1, source_target_pairs={{0,2},{2,0},{4,6},{6,4},{8,10},{10,8},{12,14},{14,12},{16,18},{18,... | collective-permute-start | bytes 786440 | tf_op jit(solution)/shard_map/ppermute | solution.py:57
  239.0 60.1 %collective-permute-start.49 = (bf16[32,576]{0,1:T(8,128)(2,1)S(1)}, bf16[32,576]{0,1:T(8,128)(2,1)S(1)}, u32[]{:S(2)}, u32[]{:S(2)}) collective-permute-start(bf16[32,576]{0,1:T(8,128)(2,1)S(1)} %get-tuple-element.224), channel_id=1, source_target_pairs={{0,28},{2,30},{4,24},{6,26},{8,20},{10,22},{12,16},{14,18},{16,12}... | collective-permute-start | bytes 110600 | tf_op jit(solution)/shard_map/ppermute | solution.py:57
  248.4 55.3 %collective-permute-start.50 = (bf16[32,576]{0,1:T(8,128)(2,1)S(1)}, bf16[32,576]{0,1:T(8,128)(2,1)S(1)}, u32[]{:S(2)}, u32[]{:S(2)}) collective-permute-start(bf16[32,576]{0,1:T(8,128)(2,1)S(1)} %get-tuple-element.223), channel_id=1, source_target_pairs={{0,30},{2,28},{4,26},{6,24},{8,22},{10,20},{12,18},{14,16},{16,14}... | collective-permute-start | bytes 110600 | tf_op jit(solution)/shard_map/ppermute | solution.py:57
  253.9 50.7 %collective-permute-start.51 = (bf16[32,576]{0,1:T(8,128)(2,1)S(1)}, bf16[32,576]{0,1:T(8,128)(2,1)S(1)}, u32[]{:S(2)}, u32[]{:S(2)}) collective-permute-start(bf16[32,576]{0,1:T(8,128)(2,1)S(1)} %get-tuple-element.222), channel_id=1, source_target_pairs={{0,24},{2,26},{4,28},{6,30},{8,16},{10,18},{12,20},{14,22},{16,8},... | collective-permute-start | bytes 110600 | tf_op jit(solution)/shard_map/ppermute | solution.py:57
  259.2 48.6 %collective-permute-start.52 = (bf16[32,576]{0,1:T(8,128)(2,1)S(1)}, bf16[32,576]{0,1:T(8,128)(2,1)}, u32[]{:S(2)}, u32[]{:S(2)}) collective-permute-start(bf16[32,576]{0,1:T(8,128)(2,1)S(1)} %get-tuple-element.221), channel_id=1, source_target_pairs={{0,26},{2,24},{4,30},{6,28},{8,18},{10,16},{12,22},{14,20},{16,10}... | collective-permute-start | bytes 110600 | tf_op jit(solution)/shard_map/ppermute | solution.py:57
  266.8 41.2 %collective-permute-start.57 = (bf16[32,576]{0,1:T(8,128)(2,1)S(1)}, bf16[32,576]{0,1:T(8,128)(2,1)}, u32[]{:S(2)}, u32[]{:S(2)}) collective-permute-start(bf16[32,576]{0,1:T(8,128)(2,1)S(1)} %get-tuple-element.220), channel_id=1, source_target_pairs={{0,18},{2,16},{4,22},{6,20},{8,26},{10,24},{12,30},{14,28},{16,2},... | collective-permute-start | bytes 110600 | tf_op jit(solution)/shard_map/ppermute | solution.py:57
  299.1 15.0 %collective-permute-start.58 = (bf16[32,576]{0,1:T(8,128)(2,1)S(1)}, bf16[32,576]{0,1:T(8,128)(2,1)S(1)}, u32[]{:S(2)}, u32[]{:S(2)}) collective-permute-start(bf16[32,576]{0,1:T(8,128)(2,1)S(1)} %get-tuple-element.219), channel_id=1, source_target_pairs={{0,22},{2,20},{4,18},{6,16},{8,30},{10,28},{12,26},{14,24},{16,6},... | collective-permute-start | bytes 110600 | tf_op jit(solution)/shard_map/ppermute | solution.py:57
  303.7 14.6 %collective-permute-start.59 = (bf16[32,576]{0,1:T(8,128)(2,1)S(1)}, bf16[32,576]{0,1:T(8,128)(2,1)S(1)}, u32[]{:S(2)}, u32[]{:S(2)}) collective-permute-start(bf16[32,576]{0,1:T(8,128)(2,1)S(1)} %get-tuple-element.218), channel_id=1, source_target_pairs={{0,16},{2,18},{4,20},{6,22},{8,24},{10,26},{12,28},{14,30},{16,0},... | collective-permute-start | bytes 110600 | tf_op jit(solution)/shard_map/ppermute | solution.py:57
  304.6 24.2 %collective-permute-start.60 = (bf16[32,576]{0,1:T(8,128)(2,1)}, bf16[32,576]{0,1:T(8,128)(2,1)}, u32[]{:S(2)}, u32[]{:S(2)}) collective-permute-start(bf16[32,576]{0,1:T(8,128)(2,1)} %get-tuple-element.217), channel_id=1, source_target_pairs={{0,20},{2,22},{4,16},{6,18},{8,28},{10,30},{12,24},{14,26},{16,4},... | collective-permute-start | bytes 110600 | tf_op jit(solution)/shard_map/ppermute | solution.py:57
  307.8 22.1 %collective-permute-start.65 = (bf16[32,576]{0,1:T(8,128)(2,1)}, bf16[32,576]{0,1:T(8,128)(2,1)}, u32[]{:S(2)}, u32[]{:S(2)}) collective-permute-start(bf16[32,576]{0,1:T(8,128)(2,1)} %get-tuple-element.216), channel_id=1, source_target_pairs={{0,12},{2,14},{4,8},{6,10},{8,4},{10,6},{12,0},{14,2},{16,28},{18,... | collective-permute-start | bytes 110600 | tf_op jit(solution)/shard_map/ppermute | solution.py:57
  308.0 22.9 %collective-permute-start.66 = (bf16[32,576]{0,1:T(8,128)(2,1)}, bf16[32,576]{0,1:T(8,128)(2,1)}, u32[]{:S(2)}, u32[]{:S(2)}) collective-permute-start(bf16[32,576]{0,1:T(8,128)(2,1)} %get-tuple-element.215), channel_id=1, source_target_pairs={{0,14},{2,12},{4,10},{6,8},{8,6},{10,4},{12,2},{14,0},{16,30},{18,... | collective-permute-start | bytes 110600 | tf_op jit(solution)/shard_map/ppermute | solution.py:57
  314.1 17.9 %collective-permute-start.67 = (bf16[32,576]{0,1:T(8,128)(2,1)S(1)}, bf16[32,576]{0,1:T(8,128)(2,1)}, u32[]{:S(2)}, u32[]{:S(2)}) collective-permute-start(bf16[32,576]{0,1:T(8,128)(2,1)S(1)} %get-tuple-element.214), channel_id=1, source_target_pairs={{0,8},{2,10},{4,12},{6,14},{8,0},{10,2},{12,4},{14,6},{16,24},{18,... | collective-permute-start | bytes 110600 | tf_op jit(solution)/shard_map/ppermute | solution.py:57
  318.3 14.8 %collective-permute-start.68 = (bf16[32,576]{0,1:T(8,128)(2,1)}, bf16[32,576]{0,1:T(8,128)(2,1)}, u32[]{:S(2)}, u32[]{:S(2)}) collective-permute-start(bf16[32,576]{0,1:T(8,128)(2,1)} %get-tuple-element.213), channel_id=1, source_target_pairs={{0,10},{2,8},{4,14},{6,12},{8,2},{10,0},{12,6},{14,4},{16,26},{18,... | collective-permute-start | bytes 110600 | tf_op jit(solution)/shard_map/ppermute | solution.py:57
  370.5 26.9 %collective-permute-start.76 = (bf16[16,216,256]{2,1,0:T(8,128)(2,1)}, bf16[16,216,256]{2,1,0:T(8,128)(2,1)S(1)}, u32[]{:S(2)}, u32[]{:S(2)}) collective-permute-start(bf16[16,216,256]{2,1,0:T(8,128)(2,1)} %dynamic-slice_bitcast_fusion), channel_id=1, source_target_pairs={{0,1},{1,0},{2,3},{3,2},{4,5},{5,4},{6,7},{7,6},{8,9},{9,8},{10,11... | collective-permute-start | bytes 5308424 | tf_op jit(solution)/shard_map/ppermute | solution.py:61
  380.5 9.5 %collective-permute-start.91 = (f32[32,48]{1,0:T(8,128)S(1)}, f32[32,48]{1,0:T(8,128)S(1)}, u32[]{:S(2)}, u32[]{:S(2)}) collective-permute-start(f32[32,48]{1,0:T(8,128)S(1)} %add.463), channel_id=1, source_target_pairs={{0,8},{2,10},{4,12},{6,14},{8,0},{10,2},{12,4},{14,6},{16,24},{18,... | collective-permute-start | bytes 18440 | tf_op jit(solution)/shard_map/ppermute | solution.py:57
  399.6 8.4 %collective-permute-start.86 = (bf16[432,256]{1,0:T(8,128)(2,1)S(1)}, bf16[432,256]{1,0:T(8,128)(2,1)S(1)}, u32[]{:S(2)}, u32[]{:S(2)}) collective-permute-start(bf16[432,256]{1,0:T(8,128)(2,1)S(1)} %pad_maximum_fusion.6), channel_id=1, source_target_pairs={{0,2},{2,0},{4,6},{6,4},{8,10},{10,8},{12,14},{14,12},{16,18},{18,... | collective-permute-start | bytes 663560 | tf_op jit(solution)/shard_map/ppermute | solution.py:57
  400.3 8.5 %collective-permute-start.83 = (bf16[432,256]{1,0:T(8,128)(2,1)S(1)}, bf16[432,256]{1,0:T(8,128)(2,1)S(1)}, u32[]{:S(2)}, u32[]{:S(2)}) collective-permute-start(bf16[432,256]{1,0:T(8,128)(2,1)S(1)} %pad_maximum_fusion.5), channel_id=1, source_target_pairs={{0,4},{2,6},{4,0},{6,2},{8,12},{10,14},{12,8},{14,10},{16,20},{18,... | collective-permute-start | bytes 663560 | tf_op jit(solution)/shard_map/ppermute | solution.py:57
  401.3 10.1 %collective-permute-start.80 = (bf16[432,256]{1,0:T(8,128)(2,1)S(1)}, bf16[432,256]{1,0:T(8,128)(2,1)S(1)}, u32[]{:S(2)}, u32[]{:S(2)}) collective-permute-start(bf16[432,256]{1,0:T(8,128)(2,1)S(1)} %pad_maximum_fusion.4), channel_id=1, source_target_pairs={{0,2},{2,0},{4,6},{6,4},{8,10},{10,8},{12,14},{14,12},{16,18},{18,... | collective-permute-start | bytes 663560 | tf_op jit(solution)/shard_map/ppermute | solution.py:57
  402.6 10.9 %collective-permute-start.77 = (bf16[432,256]{1,0:T(8,128)(2,1)S(1)}, bf16[432,256]{1,0:T(8,128)(2,1)S(1)}, u32[]{:S(2)}, u32[]{:S(2)}) collective-permute-start(bf16[432,256]{1,0:T(8,128)(2,1)S(1)} %pad_maximum_fusion.3), channel_id=1, source_target_pairs={{0,4},{2,6},{4,0},{6,2},{8,12},{10,14},{12,8},{14,10},{16,20},{18,... | collective-permute-start | bytes 663560 | tf_op jit(solution)/shard_map/ppermute | solution.py:57
  408.1 13.0 %collective-permute-start.87 = (bf16[216,256]{1,0:T(8,128)(2,1)S(1)}, bf16[216,256]{1,0:T(8,128)(2,1)S(1)}, u32[]{:S(2)}, u32[]{:S(2)}) collective-permute-start(bf16[216,256]{1,0:T(8,128)(2,1)S(1)} %slice.424), channel_id=1, source_target_pairs={{0,4},{2,6},{4,0},{6,2},{8,12},{10,14},{12,8},{14,10},{16,20},{18,... | collective-permute-start | bytes 331784 | tf_op jit(solution)/shard_map/ppermute | solution.py:57
  416.3 9.4 %collective-permute-start.82 = (bf16[216,256]{1,0:T(8,128)(2,1)S(1)}, bf16[216,256]{1,0:T(8,128)(2,1)S(1)}, u32[]{:S(2)}, u32[]{:S(2)}) collective-permute-start(bf16[216,256]{1,0:T(8,128)(2,1)S(1)} %fusion.87), channel_id=1, source_target_pairs={{0,16},{2,18},{4,20},{6,22},{8,24},{10,26},{12,28},{14,30},{16,0},... | collective-permute-start | bytes 331784 | tf_op jit(solution)/shard_map/ppermute | solution.py:57
  (91 other events, 795.1 us)
